TPU v7x, 256 devices: a whole 4x4x8 slice. The times are simulated.
256 devices in a mesh: row: 16 (over x, y_lo, core), col: 16 (over y_hi, z).
Axes of the slice: x: 4, y: 4 (y_hi: 2, y_lo: 2; y = y_hi * 2 + y_lo), z: 8, core: 2. Of those that a mesh axis runs over, the one named last changes fastest.
Arguments:
- points: bfloat16 [24576, 256], P(('row', 'col')), may hold values from -5 to 5
- mass: float32 [24576], P(('row', 'col')), may hold values from 0.05 to 20
Outputs:
- potential: float32 [24576], P(('row', 'col'))
All inputs are finite; a program needn't handle non-finite values.
Results may differ from a plain program's by a relative error of at most 0.0003.
Values may be sent and summed in bfloat16 or wider, within the bound.
No kernel may reach another device: no remote copies, remote signals or barrier semaphores. Data moves between devices by JAX's collectives and lax.ppermute only.
A program may use at most 64 MiB of HBM per device.

v0:
```python
import math

import jax
import jax.numpy as jnp
from jax import lax
from jax.sharding import PartitionSpec as P

SWEEPS = 3


epsilon_value = 0.1


def merged_2(array, axis, combine):
    everything = jax.tree.map(lambda part: lax.all_gather(part, axis), array)
    first = jax.tree.map(lambda part: part[0], everything)

    def hop(k, so_far):
        return combine(so_far, jax.tree.map(lambda part: part[k], everything))

    return lax.fori_loop(1, lax.axis_size(axis), hop, first)


def combine_lse(first_part, second_part):
    largest = jnp.maximum(first_part[0], second_part[0])
    totals = first_part[1] * jnp.exp(first_part[0] - largest) + second_part[1] * jnp.exp(
        second_part[0] - largest
    )
    return (largest, totals)


def tile_lse(left_points, right_points, right_terms):
    total_rows = left_points.shape[0]
    pieces_count = max(1, total_rows // 512)
    while total_rows % pieces_count:
        pieces_count -= 1
    block_size = total_rows // pieces_count
    left_blocks = left_points.reshape(pieces_count, block_size, left_points.shape[1])
    left_parts = jnp.zeros((pieces_count, block_size), jnp.float32)
    width_cols = right_points.shape[0]
    initial = (jnp.full((width_cols,), -1e30, jnp.float32), jnp.zeros((width_cols,), jnp.float32))

    def scan_step(column_acc, inputs):
        row_piece, row_terms = inputs
        products = (
            lax.dot_general(
                row_piece,
                right_points,
                (((1,), (1,)), ((), ())),
                preferred_element_type=jnp.float32,
            )
            / epsilon_value
        )
        scores = products + right_terms[None, :]
        largest = jnp.max(scores, axis=1)
        totals = jnp.sum(jnp.exp(scores - largest[:, None]), axis=1)
        return (column_acc, (largest, totals))

    column_acc, outputs = lax.scan(scan_step, initial, (left_blocks, left_parts))
    return ((outputs[0].reshape(total_rows), outputs[1].reshape(total_rows)), column_acc)


def full_partials(points, row_block):
    column_points = lax.all_gather(points, "row", axis=0, tiled=True)

    def partial_terms(own_terms):
        column_terms = lax.all_gather(own_terms, "row", axis=0, tiled=True)
        row_part, unused = tile_lse(row_block, column_points, column_terms)
        return (row_part, None)

    return partial_terms


def own_rows_lse(row_part, local_rows):
    offset_start = lax.axis_index("col") * local_rows
    merged = merged_2((row_part[0], row_part[1]), "col", combine_lse)
    log_sums = merged[0] + jnp.log(merged[1])
    return lax.dynamic_slice_in_dim(log_sums, offset_start, local_rows)


def shards(points, mass):
    row_block = lax.all_gather(points, "col", axis=0, tiled=True)
    local_rows = points.shape[0]
    total_points = local_rows * lax.axis_size("row") * lax.axis_size("col")
    squares = jnp.sum(jnp.square(points.astype(jnp.float32)), axis=1)
    log_weight = jnp.log(mass) - math.log(total_points)
    partial_fn = full_partials(points, row_block)
    potential = jnp.zeros((local_rows,), jnp.float32)
    for sweep_index in range(SWEEPS):
        own_terms = log_weight + potential / epsilon_value - 0.5 * squares / epsilon_value
        row_part, mirrored = partial_fn(own_terms)
        own_lse = own_rows_lse(row_part, local_rows)
        potential = 0.5 * (potential + (0.5 * squares - epsilon_value * own_lse))
    return potential / epsilon_value


def solution(mesh):
    return jax.shard_map(
        shards,
        mesh=mesh,
        in_specs=(P(("row", "col"), None), P(("row", "col"))),
        out_specs=P(("row", "col")),
        check_vma=False,
    )
```

profile of v0, /device:TPU:0, one launch (start us, length us, event | category | flops | bytes accessed | tf_op | source)
XLA Modules:
  0.0 395.6 jit_solution(7010390927447276065)
XLA Ops:
  0.0 1.3 dynamic-slice
  1.9 0.9 multiply_reduce_fusion
  2.8 0.8 subtract_dynamic-update-slice_fusion.2
  3.6 29.1 %all-reduce = f32[1536]{0:T(1024)S(1)} all-reduce(f32[1536]{0:T(1024)S(1)} %subtract_dynamic-update-slice_fusion.2), channel_id=1, replica_groups=mesh['row'=16,'col'=16] {'row'}, use_global_device_ids=true, to_apply=%add | all-reduce | flops 1536 | bytes 12288
  32.7 18.8 %all_gather.34 = bf16[1536,256]{1,0:T(8,128)(2,1)S(1)} all-gather(bf16[96,256]{1,0:T(8,128)(2,1)} %param.14), channel_id=1, replica_groups=mesh['row'=16,'col'=16] {'row'}, dimensions={0}, use_global_device_ids=true | all-gather | bytes 835584 | tf_op jit(solution)/shard_map/all_gather | solution.py:64
  51.5 48.5 %all_gather.33 = bf16[1536,256]{1,0:T(8,128)(2,1)S(1)} all-gather(bf16[96,256]{1,0:T(8,128)(2,1)} %param.14), channel_id=1, replica_groups=mesh['row'=16,'col'=16] {'col'}, dimensions={0}, use_global_device_ids=true | all-gather | bytes 835584 | tf_op jit(solution)/shard_map/all_gather | solution.py:82
  99.9 0.0 copy-start
  99.9 4.2 %while.87 = (s32[]{:T(128)}, f32[3,512]{1,0:T(4,128)S(1)}, f32[3,512]{1,0:T(4,128)S(1)}, bf16[3,512,256]{2,1,0:T(8,128)(2,1)S(1)}, bf16[1536,256]{1,0:T(8,128)(2...) while((s32[]{:T(128)}, f32[3,512]{1,0:T(4,128)S(1)}, f32[3,512]{1,0:T(4,128)S(1)}, ...), condition=%wide.region_4.5_spmd, body=%wide.region_1.4_spmd.sunk | while | flops 406584320 | bytes 7362657 | solution.py:59
  100.0 0.7 fusion.31
  100.7 0.6 exponential_reduce_fusion.6
  101.3 0.1 dynamic_update_slice.25
  101.3 0.7 fusion.31
  102.0 0.6 exponential_reduce_fusion.6
  102.7 0.1 dynamic_update_slice.25
  102.7 0.7 fusion.31
  103.4 0.6 exponential_reduce_fusion.6
  104.1 0.1 dynamic_update_slice.25
  104.1 36.1 %all-gather.1 = f32[16,1,1536]{2,1,0:T(1,128)S(1)} all-gather(f32[1,1,1536]{2,1,0:T(1,128)S(1)} %reshape.23), channel_id=1, replica_groups=mesh['row'=16,'col'=16] {'col'}, dimensions={0}, use_global_device_ids=true | all-gather | bytes 104448 | tf_op jit(solution)/shard_map/all_gather | solution.py:15
  140.2 38.0 %all-gather = f32[16,1,1536]{2,1,0:T(1,128)S(1)} all-gather(f32[1,1,1536]{2,1,0:T(1,128)S(1)} %reshape.21), channel_id=1, replica_groups=mesh['row'=16,'col'=16] {'col'}, dimensions={0}, use_global_device_ids=true | all-gather | bytes 104448 | tf_op jit(solution)/shard_map/all_gather | solution.py:15
  178.3 1.4 while.88
  179.7 0.0 copy-done
  179.7 0.2 subtract_dynamic-update-slice_fusion.1
  179.9 27.6 %all-reduce.1 = f32[1536]{0:T(1024)S(1)} all-reduce(f32[1536]{0:T(1024)S(1)} %subtract_dynamic-update-slice_fusion.1), channel_id=1, replica_groups=mesh['row'=16,'col'=16] {'row'}, use_global_device_ids=true, to_apply=%add.1 | all-reduce | flops 1536 | bytes 12288
  207.6 4.2 %while.89 = (s32[]{:T(128)}, f32[3,512]{1,0:T(4,128)S(1)}, f32[3,512]{1,0:T(4,128)S(1)}, bf16[3,512,256]{2,1,0:T(8,128)(2,1)S(1)}, bf16[1536,256]{1,0:T(8,128)(2...) while((s32[]{:T(128)}, f32[3,512]{1,0:T(4,128)S(1)}, f32[3,512]{1,0:T(4,128)S(1)}, ...), condition=%wide.region_10.11_spmd, body=%wide.region_7.10_spmd.sunk | while | flops 406584320 | bytes 7362657 | solution.py:59
  207.6 0.7 fusion.33
  208.3 0.6 exponential_reduce_fusion.7
  208.9 0.1 dynamic_update_slice.27
  209.0 0.7 fusion.33
  209.7 0.6 exponential_reduce_fusion.7
  210.3 0.1 dynamic_update_slice.27
  210.4 0.7 fusion.33
  211.1 0.6 exponential_reduce_fusion.7
  211.7 0.1 dynamic_update_slice.27
  211.8 36.1 %all-gather.3 = f32[16,1,1536]{2,1,0:T(1,128)S(1)} all-gather(f32[1,1,1536]{2,1,0:T(1,128)S(1)} %reshape.27), channel_id=1, replica_groups=mesh['row'=16,'col'=16] {'col'}, dimensions={0}, use_global_device_ids=true | all-gather | bytes 104448 | tf_op jit(solution)/shard_map/all_gather | solution.py:15
  247.9 38.0 %all-gather.2 = f32[16,1,1536]{2,1,0:T(1,128)S(1)} all-gather(f32[1,1,1536]{2,1,0:T(1,128)S(1)} %reshape.25), channel_id=1, replica_groups=mesh['row'=16,'col'=16] {'col'}, dimensions={0}, use_global_device_ids=true | all-gather | bytes 104448 | tf_op jit(solution)/shard_map/all_gather | solution.py:15
  286.0 1.4 while.90
  287.4 0.2 subtract_dynamic-update-slice_fusion
  287.6 27.6 %all-reduce.2 = f32[1536]{0:T(1024)S(1)} all-reduce(f32[1536]{0:T(1024)S(1)} %get-tuple-element.587), channel_id=1, replica_groups=mesh['row'=16,'col'=16] {'row'}, use_global_device_ids=true, to_apply=%add.2 | all-reduce | flops 1536 | bytes 12288
  315.2 4.2 %while.91 = (s32[]{:T(128)}, f32[3,512]{1,0:T(4,128)S(1)}, f32[3,512]{1,0:T(4,128)S(1)}, bf16[3,512,256]{2,1,0:T(8,128)(2,1)S(1)}, bf16[1536,256]{1,0:T(8,128)(2...) while((s32[]{:T(128)}, f32[3,512]{1,0:T(4,128)S(1)}, f32[3,512]{1,0:T(4,128)S(1)}, ...), condition=%wide.region_16.17_spmd, body=%wide.region_13.16_spmd.sunk | while | flops 406584320 | bytes 7362657 | solution.py:59
  315.3 0.7 fusion.35
  316.0 0.6 exponential_reduce_fusion.8
  316.6 0.1 dynamic_update_slice.29
  316.6 0.7 fusion.35
  317.3 0.6 exponential_reduce_fusion.8
  318.0 0.1 dynamic_update_slice.29
  318.0 0.7 fusion.35
  318.7 0.6 exponential_reduce_fusion.8
  319.4 0.1 dynamic_update_slice.29
  319.4 36.1 %all-gather.5 = f32[16,1,1536]{2,1,0:T(1,128)S(1)} all-gather(f32[1,1,1536]{2,1,0:T(1,128)S(1)} %reshape.31), channel_id=1, replica_groups=mesh['row'=16,'col'=16] {'col'}, dimensions={0}, use_global_device_ids=true | all-gather | bytes 104448 | tf_op jit(solution)/shard_map/all_gather | solution.py:15
  355.5 38.0 %all-gather.4 = f32[16,1,1536]{2,1,0:T(1,128)S(1)} all-gather(f32[1,1,1536]{2,1,0:T(1,128)S(1)} %reshape.29), channel_id=1, replica_groups=mesh['row'=16,'col'=16] {'col'}, dimensions={0}, use_global_device_ids=true | all-gather | bytes 104448 | tf_op jit(solution)/shard_map/all_gather | solution.py:15
  393.6 1.4 while.92
  395.0 0.6 add_multiply_fusion
  (126 shorter events, 3.3 us)
Async XLA Ops:
  99.9 79.8 %copy-start = (f32[96]{0:T(128)S(1)}, f32[96]{0:T(128)}, u32[]{:S(2)}) copy-start(f32[96]{0:T(128)} %param.15) | copy-start | bytes 1156
where the time goes:
time: 396 us
  blocking collectives  374 us (94%)
  other arithmetic  8.48 us (2%)
  matrix products  6.29 us (2%)
  local copies, waits for them, and re-layouts  4.37 us (1%)
    all_gather x6, blocking collectives, merged_2(): everything = jax.tree.map(lambda part: lax.all_gather(part, axis), array)  222 us
    unnamed x3, blocking collectives  84.4 us
    all_gather x1, blocking collectives, shards(): row_block = lax.all_gather(points, 'col', axis=0, tiled=True)  48.5 us
    all_gather x1, blocking collectives, full_partials(): column_points = lax.all_gather(points, 'row', axis=0, tiled=True)  18.8 us

commit v1 on v0

v1 whole, which is shorter than its diff:
```python
import jax
import jax.numpy as jnp
from jax import lax
from jax.sharding import Mesh
from jax.sharding import PartitionSpec as P

SWEEPS = 3
EPSILON = 0.1
AXES = ("x", "yl", "k", "yh", "z")
ROW = ("x", "yl", "k")
COL = ("yh", "z")


def copies(array, count):
    return jnp.broadcast_to(array[None], (count,) + array.shape)


def gathered(array, axes, count):
    return lax.all_to_all(copies(array, count), axes, 0, 0)


def mass_parts(mass):
    high = lax.reduce_precision(mass, 8, 7)
    middle = lax.reduce_precision(mass - high, 8, 7)
    low = mass - high - middle
    return jnp.stack([high, middle, low]).astype(jnp.bfloat16)


def shards(points, mass):
    own, width = points.shape
    n_row, n_col = 16, 16
    total = own * n_row * n_col
    parts = jnp.pad(mass_parts(mass), ((0, 13), (0, width - own)))
    column = gathered(jnp.concatenate([points, parts], 0), COL, n_col)
    right = column[:, :own].reshape(n_col * own, width)
    right_mass = jnp.sum(column[:, own : own + 3, :own].astype(jnp.float32), axis=1).reshape(n_col * own)
    left = gathered(points, ("x", "yl"), 8)
    left = lax.all_gather(left, "k", axis=1).reshape(n_row * own, width)
    right_squares = jnp.sum(jnp.square(right.astype(jnp.float32)), axis=1)
    left_squares = jnp.sum(jnp.square(left.astype(jnp.float32)), axis=1)
    inner = lax.dot_general(right, left, (((1,), (1,)), ((), ())), preferred_element_type=jnp.float32)
    kernel = jnp.exp((inner - 0.5 * right_squares[:, None] - 0.5 * left_squares[None, :]) / EPSILON)
    sums = jnp.sum(kernel * (right_mass / total)[:, None], axis=0)
    got = gathered(jnp.concatenate([sums, mass]), ROW, n_row)
    left_f = -0.5 * jnp.log(jnp.sum(got[:, : n_row * own], axis=0))
    left_mass = got[:, n_row * own :].reshape(n_row * own)
    left_weight = (left_mass / total) * jnp.exp(left_f)
    sums = jnp.sum(kernel * left_weight[None, :], axis=1)
    row = lax.axis_index(ROW)
    own_f = lax.dynamic_slice_in_dim(left_f, row * own, own)
    got = gathered(jnp.concatenate([sums, own_f]), COL, n_col)
    right_f = got[:, n_col * own :].reshape(n_col * own)
    right_f = 0.5 * (right_f - jnp.log(jnp.sum(got[:, : n_col * own], axis=0)))
    right_weight = (right_mass / total) * jnp.exp(right_f)
    sums = jnp.sum(kernel * right_weight[:, None], axis=0).reshape(n_row, 1, own)
    sums = jnp.sum(lax.all_to_all(sums, ROW, 0, 0), axis=(0, 1))
    col = lax.axis_index(COL)
    own_f = lax.dynamic_slice_in_dim(right_f, col * own, own)
    return 0.5 * (own_f - jnp.log(sums))


def solution(mesh):
    fine = Mesh(mesh.devices.reshape(4, 2, 2, 2, 8), AXES)
    return jax.shard_map(
        shards,
        mesh=fine,
        in_specs=(P(AXES, None), P(AXES)),
        out_specs=P(AXES),
        check_vma=False,
    )
```

time: 396 us -> 104 us (0.26)
  the two profiles are of different devices: /device:TPU:0 before, /device:TPU:1 now
where the time goes in v1:
time: 104 us
  waiting for transfers between devices  34.6 us (33%)
  starting transfers between devices  29.8 us (29%)
  blocking collectives  17.7 us (17%)
  other arithmetic  11.7 us (11%)
  matrix products  5.1 us (5%)
  local copies, waits for them, and re-layouts  4.52 us (4%)
    all_to_all x3, waiting for transfers between devices, gathered(): return lax.all_to_all(copies(array, count), axes, 0, 0)  29.1 us
    all_to_all x3, starting transfers between devices, gathered(): return lax.all_to_all(copies(array, count), axes, 0, 0)  24.6 us
    all_to_all x1, blocking collectives, gathered(): return lax.all_to_all(copies(array, count), axes, 0, 0)  13.5 us
    all_to_all x1, waiting for transfers between devices, shards(): sums = jnp.sum(lax.all_to_all(sums, ROW, 0, 0), axis=(0, 1))  5.55 us
    all_to_all x1, starting transfers between devices, shards(): sums = jnp.sum(lax.all_to_all(sums, ROW, 0, 0), axis=(0, 1))  5.12 us
    dot_general x1, matrix products, shards(): lax.dot_general(right, left, (((1,), (1,)), ((), ())), preferred_element_...  5.1 us
    reduce_sum x1, other arithmetic, shards(): sums = jnp.sum(kernel * left_weight[None, :], axis=1)  4.39 us
    reduce_sum x1, other arithmetic, shards(): jnp.sum(kernel * right_weight[:, None], axis=0).reshape(n_row, 1, own)  4.37 us
  transfers between devices with their start and end apart: 4, of which 4 were waited for; matrix products, arithmetic and copies ran while one was open for 2% of the time, Pallas kernels for 0%

profile of v1, /device:TPU:1, one launch (start us, length us, event | category | flops | bytes accessed | tf_op | source)
XLA Modules:
  0.0 103.5 jit_solution(8873600806812487839)
XLA Ops:
  0.0 1.6 %broadcast_in_dim.9 = bf16[8,96,256]{2,1,0:T(8,128)(2,1)} broadcast(bf16[96,256]{1,0:T(8,128)(2,1)} %param.2), dimensions={1,2} | broadcast | bytes 442368 | tf_op jit(solution)/shard_map/broadcast_in_dim | solution.py:15
  1.6 5.9 %all-to-all-start.1 = ((bf16[8,96,256]{2,1,0:T(8,128)(2,1)}), bf16[8,96,256]{2,1,0:T(8,128)(2,1)S(1)}, u32[]{:S(2)}, u32[]{:S(2)}) async-start(bf16[8,96,256]{2,1,0:T(8,128)(2,1)} %broadcast_in_dim.9), calls=%async_computation.1 | async-start | bytes 786432 | tf_op jit(solution)/shard_map/all_to_all | solution.py:19
  7.4 0.7 fusion.12
  8.1 0.8 pad_maximum_fusion
  8.9 5.7 %all-to-all-done.1 = bf16[8,96,256]{2,1,0:T(8,128)(2,1)S(1)} async-done(((bf16[8,96,256]{2,1,0:T(8,128)(2,1)}), bf16[8,96,256]{2,1,0:T(8,128)(2,1)S(1)}, u32[]{:S(2)}, u32[]{:S(2)}) %all-to-all-start.1) | async-done | bytes 393248 | tf_op jit(solution)/shard_map/all_to_all | solution.py:19
  14.6 1.0 broadcast_in_dim.8
  15.6 10.6 %all-to-all-start = ((bf16[16,112,256]{2,1,0:T(8,128)(2,1)}), bf16[16,112,256]{2,1,0:T(8,128)(2,1)S(1)}, u32[]{:S(2)}, u32[]{:S(2)}) async-start(bf16[16,112,256]{2,1,0:T(8,128)(2,1)} %broadcast_in_dim.8), calls=%async_computation | async-start | bytes 1835008 | tf_op jit(solution)/shard_map/all_to_all | solution.py:19
  26.2 4.2 %all-gather = bf16[8,192,256]{2,1,0:T(8,128)(2,1)S(1)} all-gather(bf16[8,96,256]{2,1,0:T(8,128)(2,1)S(1)} %all-to-all-done.1), channel_id=2, replica_groups=mesh['x'=4,'yl'=2,'k'=2,'yh'=2,'z'=8] {'k'}, dimensions={1}, use_global_device_ids=true | all-gather | bytes 1179648 | tf_op jit(solution)/shard_map/all_gather | solution.py:38
  30.4 0.4 multiply_reduce_fusion.3
  30.8 0.1 mul.112
  30.9 17.4 %all-to-all-done = bf16[16,112,256]{2,1,0:T(8,128)(2,1)S(1)} async-done(((bf16[16,112,256]{2,1,0:T(8,128)(2,1)}), bf16[16,112,256]{2,1,0:T(8,128)(2,1)S(1)}, u32[]{:S(2)}, u32[]{:S(2)}) %all-to-all-start) | async-done | bytes 917536 | tf_op jit(solution)/shard_map/all_to_all | solution.py:19
  48.3 0.1 div.20
  48.4 0.3 multiply_reduce_fusion.4
  48.8 0.1 mul.109
  48.8 0.1 slice.24
  48.9 0.0 copy-start
  48.9 5.1 %multiply_reduce_fusion.2 = (f32[1536]{0:T(1024)S(1)}, f32[1536,1536]{1,0:T(8,128)}) fusion(f32[1536]{0:T(1024)S(1)} %div.20, f32[1536]{0:T(1024)S(1)} %mul.112, f32[1536]{0:T(1024)S(1)} %mul.109, bf16[1536,256]{1,0:T(8,128)(2,1)S(1)} %bitcast.18, bf16[1536,256]{1,0:T(8,128)(2,1)S(1)} %bitcast.17), kind=kOutput, calls=%fused_computation.5 | convolution fusion | flops 1219754496 | bytes 11034624 | tf_op jit(solution)/shard_map/dot_general | solution.py:41
  54.0 0.0 copy-done
  54.0 0.7 broadcast_in_dim.10
  54.7 8.2 %all-to-all-start.2 = ((f32[16,1,1632]{2,1,0:T(1,128)}), f32[16,1,1632]{2,1,0:T(1,128)S(1)}, u32[]{:S(2)}, u32[]{:S(2)}) async-start(f32[16,1,1632]{2,1,0:T(1,128)} %broadcast_in_dim.10), calls=%async_computation.2 | async-start | bytes 212992 | tf_op jit(solution)/shard_map/all_to_all | solution.py:19
  62.9 6.0 %all-to-all-done.2 = f32[16,1,1632]{2,1,0:T(1,128)S(1)} async-done(((f32[16,1,1632]{2,1,0:T(1,128)}), f32[16,1,1632]{2,1,0:T(1,128)S(1)}, u32[]{:S(2)}, u32[]{:S(2)}) %all-to-all-start.2) | async-done | bytes 104480 | tf_op jit(solution)/shard_map/all_to_all | solution.py:19
  68.9 0.1 div.22
  69.0 0.1 dynamic_slice.6
  69.1 4.4 %multiply_reduce_fusion.1 = f32[1536]{0:T(1024)S(1)} fusion(f32[1536,1536]{1,0:T(8,128)} %get-tuple-element.13, f32[1536]{0:T(1024)S(1)} %get-tuple-element.7), kind=kLoop, calls=%fused_computation.4 | loop fusion | flops 4717056 | bytes 9449472 | tf_op jit(solution)/shard_map/reduce_sum | solution.py:48
  73.5 0.1 broadcast_in_dim.11
  73.5 13.5 %all_to_all.33 = f32[16,1,1632]{2,1,0:T(1,128)S(1)} all-to-all(f32[16,1,1632]{2,1,0:T(1,128)S(1)} %broadcast_in_dim.11), channel_id=1, replica_groups=mesh['x'=4,'yl'=2,'k'=2,'yh'=2,'z'=8] {'yh','z'}, dimensions={0} | all-to-all | bytes 208896 | tf_op jit(solution)/shard_map/all_to_all | solution.py:19
  87.1 0.1 reshape.84
  87.2 4.4 %multiply_reduce_fusion = f32[1536]{0:T(1024)S(1)} fusion(f32[1536,1536]{1,0:T(8,128)} %get-tuple-element.13, f32[1536]{0:T(1024)S(1)} %get-tuple-element.5), kind=kLoop, calls=%fused_computation.3 | loop fusion | flops 4717056 | bytes 9449472 | tf_op jit(solution)/shard_map/reduce_sum | solution.py:55
  91.6 0.7 reshape.85
  92.3 5.1 %all-to-all-start.4 = ((f32[16,1,96]{2,1,0:T(1,128)}), f32[16,1,96]{2,1,0:T(1,128)S(1)}, u32[]{:S(2)}, u32[]{:S(2)}) async-start(f32[16,1,96]{2,1,0:T(1,128)} %reshape.85), calls=%async_computation.4 | async-start | bytes 16384 | tf_op jit(solution)/shard_map/all_to_all | solution.py:56
  97.4 5.5 %all-to-all-done.4 = f32[16,1,96]{2,1,0:T(1,128)S(1)} async-done(((f32[16,1,96]{2,1,0:T(1,128)}), f32[16,1,96]{2,1,0:T(1,128)S(1)}, u32[]{:S(2)}, u32[]{:S(2)}) %all-to-all-start.4) | async-done | bytes 6176 | tf_op jit(solution)/shard_map/all_to_all | solution.py:56
  102.9 0.6 subtract_multiply_fusion.1
  (17 shorter events, 0.2 us)
Async XLA Ops:
  1.6 13.0 %all-to-all-start.1 = ((bf16[8,96,256]{2,1,0:T(8,128)(2,1)}), bf16[8,96,256]{2,1,0:T(8,128)(2,1)S(1)}, u32[]{:S(2)}, u32[]{:S(2)}) async-start(bf16[8,96,256]{2,1,0:T(8,128)(2,1)} %broadcast_in_dim.9), calls=%async_computation.1 | async-start | bytes 786432 | tf_op jit(solution)/shard_map/all_to_all | solution.py:19
  15.6 32.7 %all-to-all-start = ((bf16[16,112,256]{2,1,0:T(8,128)(2,1)}), bf16[16,112,256]{2,1,0:T(8,128)(2,1)S(1)}, u32[]{:S(2)}, u32[]{:S(2)}) async-start(bf16[16,112,256]{2,1,0:T(8,128)(2,1)} %broadcast_in_dim.8), calls=%async_computation | async-start | bytes 1835008 | tf_op jit(solution)/shard_map/all_to_all | solution.py:19
  48.9 5.1 %copy-start = (f32[96]{0:T(128)S(1)}, f32[96]{0:T(128)}, u32[]{:S(2)}) copy-start(f32[96]{0:T(128)} %param.3) | copy-start | bytes 1156
  54.7 14.1 %all-to-all-start.2 = ((f32[16,1,1632]{2,1,0:T(1,128)}), f32[16,1,1632]{2,1,0:T(1,128)S(1)}, u32[]{:S(2)}, u32[]{:S(2)}) async-start(f32[16,1,1632]{2,1,0:T(1,128)} %broadcast_in_dim.10), calls=%async_computation.2 | async-start | bytes 212992 | tf_op jit(solution)/shard_map/all_to_all | solution.py:19
  92.3 10.7 %all-to-all-start.4 = ((f32[16,1,96]{2,1,0:T(1,128)}), f32[16,1,96]{2,1,0:T(1,128)S(1)}, u32[]{:S(2)}, u32[]{:S(2)}) async-start(f32[16,1,96]{2,1,0:T(1,128)} %reshape.85), calls=%async_computation.4 | async-start | bytes 16384 | tf_op jit(solution)/shard_map/all_to_all | solution.py:56

commit v2 on v1

v2 whole, which is shorter than its diff:
```python
import functools
import math

import jax
import jax.numpy as jnp
from jax import lax
from jax.experimental import pallas as pl
from jax.experimental.pallas import tpu as pltpu
from jax.sharding import Mesh
from jax.sharding import PartitionSpec as P

EPSILON = 0.1
AXES = ("x", "yl", "k", "yh", "z")
ROW = ("x", "yl", "k")
COL = ("yh", "z")
LANES = 128
STEP = 256
SCALE = math.log2(math.e) / EPSILON
VMEM = pl.BlockSpec(memory_space=pltpu.VMEM)
SMEM = pl.BlockSpec(memory_space=pltpu.SMEM)
PARAMS = pltpu.CompilerParams(vmem_limit_bytes=40 * 2**20)


def lane_pieces(length):
    return [slice(n, n + LANES) for n in range(0, length, LANES)]


def store_columns(row, columns_ref):
    for piece in lane_pieces(row.shape[1]):
        columns_ref[piece, :] = jnp.broadcast_to(row[:, piece], (LANES, LANES)).T


def repeated(column, length):
    return jnp.concatenate([column] * (length // LANES), axis=1)


def row_of_sums(partial_ref):
    return jnp.concatenate(
        [jnp.sum(partial_ref[piece, :].T, axis=0, keepdims=True) for piece in lane_pieces(partial_ref.shape[0])],
        axis=1,
    )


def copies_kernel(points_ref, mass_ref, send_ref):
    own, width = points_ref.shape
    mass = mass_ref[...]
    high = mass.astype(jnp.bfloat16).astype(jnp.float32)
    middle = (mass - high).astype(jnp.bfloat16).astype(jnp.float32)
    low = mass - high - middle
    parts = jnp.concatenate([high, middle, low, jnp.zeros((5, own), jnp.float32)], axis=0)
    parts = jnp.concatenate([parts, jnp.zeros((8, width - own), jnp.float32)], axis=1)
    block = jnp.concatenate([points_ref[...].astype(jnp.float32), parts], axis=0).astype(jnp.bfloat16)
    for d in range(send_ref.shape[0]):
        send_ref[d] = block


def left_kernel(rank_ref, near_ref, far_ref, left_ref, squares_ref, partial):
    rank = rank_ref[0]
    for core, ref in enumerate((near_ref, far_ref)):
        for y in range(2):
            for x in range(4):
                place = rank ^ (4 * x + 2 * y + core)
                block = ref[2 * x + y]
                left_ref[place] = block
                wide = block.astype(jnp.float32)
                partial[place] = wide[:, :LANES] * wide[:, :LANES] + wide[:, LANES:] * wide[:, LANES:]
    flat = partial.reshape(partial.shape[0] * partial.shape[1], LANES)
    squares_ref[...] = (-0.5 * SCALE) * row_of_sums(flat)


def concatenated(ref, start, size):
    return jnp.concatenate([ref[d, :, start : start + size] for d in range(ref.shape[0])], axis=1)


def build_kernel(total, column_ref, left_ref, squares_ref, mass_ref, kernel_ref, send_ref, weight_ref, right, columns):
    groups, own = left_ref.shape[0], left_ref.shape[1]
    length = groups * own
    masses = []
    for d in range(groups):
        right[d * own : (d + 1) * own, :] = column_ref[d, :own, :]
        parts = column_ref[d].astype(jnp.float32)[own : own + 3, :own]
        masses.append(jnp.sum(parts, axis=0, keepdims=True))
    weight = jnp.concatenate(masses, axis=1) * (1.0 / total)
    weight_ref[...] = weight
    store_columns(weight, columns)
    left = left_ref[...].reshape(length, left_ref.shape[2])
    left_squares = squares_ref[...]

    def step(n, sums):
        rows = pl.ds(pl.multiple_of(n * STEP, STEP), STEP)
        block = right[rows, :]
        wide = block.astype(jnp.float32)
        right_squares = (-0.5 * SCALE) * jnp.sum(wide * wide, axis=1, keepdims=True)
        inner = lax.dot_general(block, left, (((1,), (1,)), ((), ())), preferred_element_type=jnp.float32)
        entries = jnp.exp2(SCALE * inner + right_squares + left_squares)
        kernel_ref[rows, :] = entries
        weighted = entries * repeated(columns[rows, :], length)
        return sums + jnp.sum(weighted.reshape(STEP // 8, 8, length), axis=0)

    sums = lax.fori_loop(0, length // STEP, step, jnp.zeros((8, length), jnp.float32))
    sums = jnp.sum(sums, axis=0, keepdims=True)
    send = jnp.concatenate([sums, mass_ref[...], jnp.zeros((1, LANES - own), jnp.float32)], axis=1)
    for d in range(groups):
        send_ref[d] = send


def row_sums_kernel(total, own, rank_ref, kernel_ref, got_ref, send_ref, partial):
    groups = got_ref.shape[0]
    length = groups * own
    sums = jnp.sum(got_ref[:, :, :length], axis=0)
    potential = -0.5 * jnp.log(sums)
    mass = concatenated(got_ref, length, own)
    weight = (mass * (1.0 / total)) * jnp.exp(potential)

    def step(n, carry):
        rows = pl.ds(pl.multiple_of(n * 64, 64), 64)
        weighted = kernel_ref[rows, :] * weight
        partial[rows, :] = sum(weighted[:, piece] for piece in lane_pieces(length))
        return carry

    lax.fori_loop(0, length // 64, step, 0)
    mine = jnp.zeros((1, own), jnp.float32)
    for d in range(groups):
        mine = mine + jnp.where(rank_ref[0] == d, potential[:, d * own : (d + 1) * own], 0.0)
    pad = jnp.zeros((1, LANES - own), jnp.float32)
    send = jnp.concatenate([row_of_sums(partial), mine, pad], axis=1)
    for d in range(groups):
        send_ref[d] = send


def column_sums_kernel(own, rank_ref, kernel_ref, got_ref, weight_ref, send_ref, mine_ref, columns):
    groups = got_ref.shape[0]
    length = groups * own
    sums = jnp.sum(got_ref[:, :, :length], axis=0)
    potential = 0.5 * (concatenated(got_ref, length, own) - jnp.log(sums))
    store_columns(weight_ref[...] * jnp.exp(potential), columns)

    def step(n, sums):
        rows = pl.ds(pl.multiple_of(n * 64, 64), 64)
        weighted = kernel_ref[rows, :] * repeated(columns[rows, :], length)
        return sums + jnp.sum(weighted.reshape(8, 8, length), axis=0)

    sums = lax.fori_loop(0, length // 64, step, jnp.zeros((8, length), jnp.float32))
    sums = jnp.sum(sums, axis=0, keepdims=True)
    mine = jnp.zeros((1, own), jnp.float32)
    for d in range(groups):
        mine = mine + jnp.where(rank_ref[1] == d, potential[:, d * own : (d + 1) * own], 0.0)
        send_ref[d, :, :own] = sums[:, d * own : (d + 1) * own]
    mine_ref[...] = mine


def shards(points, mass):
    own, width = points.shape
    groups = 16
    length = groups * own
    total = length * groups
    f32 = jnp.float32
    ranks = jnp.stack([lax.axis_index(ROW), lax.axis_index(COL)]).astype(jnp.int32)
    mass = mass.reshape(1, own)
    send = pl.pallas_call(
        copies_kernel,
        out_shape=jax.ShapeDtypeStruct((groups, own + 8, width), points.dtype),
        in_specs=[VMEM, VMEM],
        out_specs=VMEM,
        compiler_params=PARAMS,
    )(points, mass)
    column = lax.all_to_all(send, COL, 0, 0)
    swap = lambda size, by: [(i, i ^ by) for i in range(size)]
    near = jnp.stack([points, lax.ppermute(points, "yl", swap(2, 1))])
    near = jnp.concatenate([near] + [lax.ppermute(near, "x", swap(4, s)) for s in (1, 2, 3)])
    far = lax.ppermute(near, "k", swap(2, 1))
    left, left_squares = pl.pallas_call(
        left_kernel,
        out_shape=[jax.ShapeDtypeStruct((groups, own, width), points.dtype), jax.ShapeDtypeStruct((1, length), f32)],
        in_specs=[SMEM, VMEM, VMEM],
        out_specs=[VMEM, VMEM],
        scratch_shapes=[pltpu.VMEM((groups, own, LANES), f32)],
        compiler_params=PARAMS,
    )(ranks, near, far)
    message = jax.ShapeDtypeStruct((groups, 1, length + LANES), f32)
    kernel, send, weight = pl.pallas_call(
        functools.partial(build_kernel, total),
        out_shape=[jax.ShapeDtypeStruct((length, length), f32), message, jax.ShapeDtypeStruct((1, length), f32)],
        in_specs=[VMEM] * 4,
        out_specs=[VMEM] * 3,
        scratch_shapes=[pltpu.VMEM((length, width), points.dtype), pltpu.VMEM((length, LANES), f32)],
        compiler_params=PARAMS,
    )(column, left, left_squares, mass)
    got = lax.all_to_all(send, ROW, 0, 0)
    send = pl.pallas_call(
        functools.partial(row_sums_kernel, total, own),
        out_shape=message,
        in_specs=[SMEM, VMEM, VMEM],
        out_specs=VMEM,
        scratch_shapes=[pltpu.VMEM((length, LANES), f32)],
        compiler_params=PARAMS,
    )(ranks, kernel, got)
    got = lax.all_to_all(send, COL, 0, 0)
    send, mine = pl.pallas_call(
        functools.partial(column_sums_kernel, own),
        out_shape=[jax.ShapeDtypeStruct((groups, 1, own), f32), jax.ShapeDtypeStruct((1, own), f32)],
        in_specs=[SMEM, VMEM, VMEM, VMEM],
        out_specs=[VMEM, VMEM],
        scratch_shapes=[pltpu.VMEM((length, LANES), f32)],
        compiler_params=PARAMS,
    )(ranks, kernel, got, weight)
    sums = jnp.sum(lax.all_to_all(send, ROW, 0, 0), axis=0)
    return (0.5 * (mine - jnp.log(sums))).reshape(own)


def solution(mesh):
    fine = Mesh(mesh.devices.reshape(4, 2, 2, 2, 8), AXES)
    return jax.shard_map(
        shards,
        mesh=fine,
        in_specs=(P(AXES, None), P(AXES)),
        out_specs=P(AXES),
        check_vma=False,
    )
```

time: 104 us -> 82.4 us (0.79)
  waiting for transfers between devices: 34.6 us -> 12.8 us
  blocking collectives: 17.7 us -> 36.6 us
  starting transfers between devices: 29.8 us -> 18.4 us
  Pallas kernels: 0 us -> 10.5 us
  other arithmetic: 11.7 us -> 1.44 us
  matrix products: 5.1 us -> 0 us
  local copies, waits for them, and re-layouts: 4.52 us -> 2.17 us
    all_to_all x4 -> x1, waiting for transfers between devices: 34.6 us -> 4.03 us  [shards(): column = lax.all_to_all(send, COL, 0, 0)]
    all_to_all x1 -> x3, blocking collectives: 13.5 us -> 36.6 us  [the longest x1 13.9 us: shards(): got = lax.all_to_all(send, COL, 0, 0)]
    all_to_all x4 -> x1, starting transfers between devices: 29.8 us -> 11.7 us  [shards(): column = lax.all_to_all(send, COL, 0, 0)]
    pallas_call x0 -> x5, Pallas kernels: none -> 10.5 us  [the longest x1 4.01 us: shards(): pl.pallas_call(functools.partial(build_kernel, total), out_shape=[jax.Sha...]
    reduce_sum x8 -> x1, other arithmetic: 9.53 us -> 0.04 us  [shards(): sums = jnp.sum(lax.all_to_all(send, ROW, 0, 0), axis=0)]
    ppermute x0 -> x5, waiting for transfers between devices: none -> 8.73 us  [the longest x3 4.52 us: shards(): lax.ppermute(near, 'x', swap(4, s))]
    ppermute x0 -> x5, starting transfers between devices: none -> 6.65 us  [the longest x3 3.34 us: shards(): lax.ppermute(near, 'x', swap(4, s))]
    dot_general x1 -> x0, matrix products: 5.1 us -> none  [shards(): lax.dot_general(right, left, (((1,), (1,)), ((), ())), preferred_element_...]
  transfers between devices with their start and end apart: 4 -> 6, of which waited for: 4 -> 5; matrix products, arithmetic and copies ran while one was open for 2% -> 2% of each run, Pallas kernels for 0% -> 1%
where the time goes in v2:
time: 82.4 us; the launch traced here: 81.9 us
  blocking collectives  36.6 us (44%)
  starting transfers between devices  18.4 us (22%)
  waiting for transfers between devices  12.8 us (16%)
  Pallas kernels  10.5 us (13%)
  local copies, waits for them, and re-layouts  2.17 us (3%)
  other arithmetic  1.44 us (2%)
    all_to_all x1, blocking collectives, shards(): got = lax.all_to_all(send, COL, 0, 0)  13.9 us
    all_to_all x1, blocking collectives, shards(): got = lax.all_to_all(send, ROW, 0, 0)  12.9 us
    all_to_all x1, starting transfers between devices, shards(): column = lax.all_to_all(send, COL, 0, 0)  11.7 us
    all_to_all x1, blocking collectives, shards(): sums = jnp.sum(lax.all_to_all(send, ROW, 0, 0), axis=0)  9.77 us
    ppermute x3, waiting for transfers between devices, shards(): lax.ppermute(near, 'x', swap(4, s))  4.52 us
    all_to_all x1, waiting for transfers between devices, shards(): column = lax.all_to_all(send, COL, 0, 0)  4.03 us
    pallas_call x1, Pallas kernels, shards(): pl.pallas_call(functools.partial(build_kernel, total), out_shape=[jax.Sha...  4.01 us
    ppermute x3, starting transfers between devices, shards(): lax.ppermute(near, 'x', swap(4, s))  3.34 us
  transfers between devices with their start and end apart: 6, of which 5 were waited for; matrix products, arithmetic and copies ran while one was open for 2% of the time, Pallas kernels for 1%

profile of v2, /device:TPU:1, one launch (start us, length us, event | category | flops | bytes accessed | tf_op | source)
XLA Modules:
  0.0 81.9 jit_solution(7605851591259061845)
XLA Ops:
  0.0 0.0 copy-start
  0.0 0.7 copy-done
  0.7 1.8 %shard_map.28 = bf16[16,104,256]{2,1,0:T(8,128)(2,1)} custom-call(bf16[96,256]{1,0:T(8,128)(2,1)} %points_ref.1, f32[1,96]{1,0:T(1,128)S(1)} %bitcast.15), custom_call_target="tpu_custom_call" | custom-call | tf_op jit(solution)/shard_map/pallas_call | solution.py:160
  2.4 11.7 %all-to-all-start = ((bf16[16,104,256]{2,1,0:T(8,128)(2,1)}), bf16[16,104,256]{2,1,0:T(8,128)(2,1)S(1)}, u32[]{:S(2)}, u32[]{:S(2)}) async-start(bf16[16,104,256]{2,1,0:T(8,128)(2,1)} %shard_map.28), calls=%async_computation | async-start | bytes 1703936 | tf_op jit(solution)/shard_map/all_to_all | solution.py:167
  14.2 0.5 collective-permute-start
  14.7 0.8 %constant_dynamic-update-slice_fusion.4 = bf16[8,96,256]{2,1,0:T(8,128)(2,1)S(1)} fusion(bf16[96,256]{1,0:T(8,128)(2,1)} %points_ref.1), kind=kLoop, calls=%fused_computation.5 | loop fusion | bytes 98304
  15.5 2.9 %collective-permute-done = bf16[96,256]{1,0:T(8,128)(2,1)S(1)} collective-permute-done((bf16[96,256]{1,0:T(8,128)(2,1)}, bf16[96,256]{1,0:T(8,128)(2,1)S(1)}, u32[]{:S(2)}, u32[]{:S(2)}) %collective-permute-start) | collective-permute-done | bytes 49184 | tf_op jit(solution)/shard_map/ppermute | solution.py:169
  18.4 0.8 pad_maximum_fusion
  19.3 2.6 %collective-permute-start.3 = (bf16[2,96,256]{2,1,0:T(8,128)(2,1)S(1)}, bf16[2,96,256]{2,1,0:T(8,128)(2,1)S(1)}, u32[]{:S(2)}, u32[]{:S(2)}) collective-permute-start(bf16[2,96,256]{2,1,0:T(8,128)(2,1)S(1)} %pad_maximum_fusion), channel_id=1, source_target_pairs={{0,192},{64,128},{128,64},{192,0},{1,193},{65,129},{129,65},{193,1... | collective-permute-start | bytes 294920 | tf_op jit(solution)/shard_map/ppermute | solution.py:170
  21.8 0.5 collective-permute-start.2
  22.3 0.3 collective-permute-start.1
  22.6 3.5 %collective-permute-done.1 = bf16[2,96,256]{2,1,0:T(8,128)(2,1)S(1)} collective-permute-done((bf16[2,96,256]{2,1,0:T(8,128)(2,1)S(1)}, bf16[2,96,256]{2,1,0:T(8,128)(2,1)S(1)}, u32[]{:S(2)}, u32[]{:S(2)}) %collective-permute-start.1) | collective-permute-done | bytes 98336 | tf_op jit(solution)/shard_map/ppermute | solution.py:170
  26.1 1.0 %collective-permute-done.2 = bf16[2,96,256]{2,1,0:T(8,128)(2,1)S(1)} collective-permute-done((bf16[2,96,256]{2,1,0:T(8,128)(2,1)S(1)}, bf16[2,96,256]{2,1,0:T(8,128)(2,1)S(1)}, u32[]{:S(2)}, u32[]{:S(2)}) %collective-permute-start.2) | collective-permute-done | bytes 98336 | tf_op jit(solution)/shard_map/ppermute | solution.py:170
  27.1 0.0 collective-permute-done.3
  27.2 2.8 %collective-permute-start.4 = (bf16[8,96,256]{2,1,0:T(8,128)(2,1)S(1)}, bf16[8,96,256]{2,1,0:T(8,128)(2,1)S(1)}, u32[]{:S(2)}, u32[]{:S(2)}) collective-permute-start(bf16[8,96,256]{2,1,0:T(8,128)(2,1)S(1)} %constant_dynamic-update-slice_fusion.near_ref), channel_id=1, source_target_pairs={{0,16},{16,0},{1,17},{17,1},{2,18},{18,2},{3,19},{19,3},{4,20},{20... | collective-permute-start | bytes 1179656 | tf_op jit(solution)/shard_map/ppermute | solution.py:171
  30.0 0.1 pad_add_fusion.rank_ref
  30.1 1.3 %collective-permute-done.4.far_ref = bf16[8,96,256]{2,1,0:T(8,128)(2,1)S(1)} collective-permute-done((bf16[8,96,256]{2,1,0:T(8,128)(2,1)S(1)}, bf16[8,96,256]{2,1,0:T(8,128)(2,1)S(1)}, u32[]{:S(2)}, u32[]{:S(2)}) %collective-permute-start.4) | collective-permute-done | bytes 393248 | tf_op jit(solution)/shard_map/ppermute | solution.py:171
  31.3 1.0 %shard_map.29 = (bf16[16,96,256]{2,1,0:T(8,128)(2,1)S(1)}, f32[1,1536]{1,0:T(1,128)S(1)}) custom-call(s32[2]{0:T(128)S(1)} %pad_add_fusion.rank_ref, bf16[8,96,256]{2,1,0:T(8,128)(2,1)S(1)} %constant_dynamic-update-slice_fusion.near_ref, bf16[8,96,256]{2,1,0:T(8,128)(2,1)S(1)} %collective-permute-done.4.far_ref), custom_call_target="tpu_custom_call" | custom-call | tf_op jit(solution)/shard_map/pallas_call | solution.py:172
  32.4 4.0 %all-to-all-done.column_ref = bf16[16,104,256]{2,1,0:T(8,128)(2,1)S(1)} async-done(((bf16[16,104,256]{2,1,0:T(8,128)(2,1)}), bf16[16,104,256]{2,1,0:T(8,128)(2,1)S(1)}, u32[]{:S(2)}, u32[]{:S(2)}) %all-to-all-start) | async-done | bytes 852000 | tf_op jit(solution)/shard_map/all_to_all | solution.py:167
  36.4 0.0 copy-start.1
  36.4 0.7 copy-done.1
  37.0 4.0 %shard_map.30 = (f32[1536,1536]{1,0:T(8,128)S(1)}, f32[16,1,1664]{2,1,0:T(1,128)S(1)}, f32[1,1536]{1,0:T(1,128)S(1)}) custom-call(bf16[16,104,256]{2,1,0:T(8,128)(2,1)S(1)} %all-to-all-done.column_ref, bf16[16,96,256]{2,1,0:T(8,128)(2,1)S(1)} %get-tuple-element.12.left_ref, f32[1,1536]{1,0:T(1,128)S(1)} %get-tuple-element.13.squares_ref, f32[1,96]{1,0:T(1,128)S(1)} %bitcast.16), custom_call_target="tpu_custom_call" | custom-call | tf_op jit(solution)/shard_map/pallas_call | solution.py:181
  41.1 12.9 %all_to_all.20.got_ref = f32[16,1,1664]{2,1,0:T(1,128)S(1)} all-to-all(f32[16,1,1664]{2,1,0:T(1,128)S(1)} %get-tuple-element.15), channel_id=1, replica_groups=mesh['x'=4,'yl'=2,'k'=2,'yh'=2,'z'=8] {'x','yl','k'}, dimensions={0} | all-to-all | bytes 212992 | tf_op jit(solution)/shard_map/all_to_all | solution.py:189
  54.0 1.8 %shard_map.31 = f32[16,1,1664]{2,1,0:T(1,128)S(1)} custom-call(s32[2]{0:T(128)S(1)} %pad_add_fusion.rank_ref, f32[1536,1536]{1,0:T(8,128)S(1)} %get-tuple-element.14.kernel_ref, f32[16,1,1664]{2,1,0:T(1,128)S(1)} %all_to_all.20.got_ref), custom_call_target="tpu_custom_call" | custom-call | tf_op jit(solution)/shard_map/pallas_call | solution.py:190
  55.8 13.9 %all_to_all.21.got_ref = f32[16,1,1664]{2,1,0:T(1,128)S(1)} all-to-all(f32[16,1,1664]{2,1,0:T(1,128)S(1)} %shard_map.31), channel_id=1, replica_groups=mesh['x'=4,'yl'=2,'k'=2,'yh'=2,'z'=8] {'yh','z'}, dimensions={0} | all-to-all | bytes 212992 | tf_op jit(solution)/shard_map/all_to_all | solution.py:198
  69.7 1.9 %shard_map.32 = (f32[16,1,96]{2,1,0:T(1,128)S(1)}, f32[1,96]{1,0:T(1,128)S(1)}) custom-call(s32[2]{0:T(128)S(1)} %pad_add_fusion.rank_ref, f32[1536,1536]{1,0:T(8,128)S(1)} %get-tuple-element.14.kernel_ref, f32[16,1,1664]{2,1,0:T(1,128)S(1)} %all_to_all.21.got_ref, f32[1,1536]{1,0:T(1,128)S(1)} %get-tuple-element.16.weight_ref), custom_call_target="tpu_custom_call" | custom-call | tf_op jit(solution)/shard_map/pallas_call | solution.py:199
  71.6 9.8 %all_to_all.22 = f32[16,1,96]{2,1,0:T(1,128)S(1)} all-to-all(f32[16,1,96]{2,1,0:T(1,128)S(1)} %get-tuple-element.18), channel_id=1, replica_groups=mesh['x'=4,'yl'=2,'k'=2,'yh'=2,'z'=8] {'x','yl','k'}, dimensions={0} | all-to-all | bytes 12288 | tf_op jit(solution)/shard_map/all_to_all | solution.py:207
  81.4 0.5 fusion.1
  (5 shorter events, 0.1 us)
Async XLA Ops:
  0.0 0.7 copy-start
  2.4 34.0 %all-to-all-start = ((bf16[16,104,256]{2,1,0:T(8,128)(2,1)}), bf16[16,104,256]{2,1,0:T(8,128)(2,1)S(1)}, u32[]{:S(2)}, u32[]{:S(2)}) async-start(bf16[16,104,256]{2,1,0:T(8,128)(2,1)} %shard_map.28), calls=%async_computation | async-start | bytes 1703936 | tf_op jit(solution)/shard_map/all_to_all | solution.py:167
  14.2 4.3 %collective-permute-start = (bf16[96,256]{1,0:T(8,128)(2,1)}, bf16[96,256]{1,0:T(8,128)(2,1)S(1)}, u32[]{:S(2)}, u32[]{:S(2)}) collective-permute-start(bf16[96,256]{1,0:T(8,128)(2,1)} %points_ref.1), channel_id=1, source_target_pairs={{0,32},{32,0},{1,33},{33,1},{2,34},{34,2},{3,35},{35,3},{4,36},{36... | collective-permute-start | bytes 147464 | tf_op jit(solution)/shard_map/ppermute | solution.py:169
  19.3 7.9 %collective-permute-start.3 = (bf16[2,96,256]{2,1,0:T(8,128)(2,1)S(1)}, bf16[2,96,256]{2,1,0:T(8,128)(2,1)S(1)}, u32[]{:S(2)}, u32[]{:S(2)}) collective-permute-start(bf16[2,96,256]{2,1,0:T(8,128)(2,1)S(1)} %pad_maximum_fusion), channel_id=1, source_target_pairs={{0,192},{64,128},{128,64},{192,0},{1,193},{65,129},{129,65},{193,1... | collective-permute-start | bytes 294920 | tf_op jit(solution)/shard_map/ppermute | solution.py:170
  21.8 5.3 %collective-permute-start.2 = (bf16[2,96,256]{2,1,0:T(8,128)(2,1)S(1)}, bf16[2,96,256]{2,1,0:T(8,128)(2,1)S(1)}, u32[]{:S(2)}, u32[]{:S(2)}) collective-permute-start(bf16[2,96,256]{2,1,0:T(8,128)(2,1)S(1)} %pad_maximum_fusion), channel_id=1, source_target_pairs={{0,128},{64,192},{128,0},{192,64},{1,129},{65,193},{129,1},{193,65... | collective-permute-start | bytes 294920 | tf_op jit(solution)/shard_map/ppermute | solution.py:170
  22.3 3.8 %collective-permute-start.1 = (bf16[2,96,256]{2,1,0:T(8,128)(2,1)S(1)}, bf16[2,96,256]{2,1,0:T(8,128)(2,1)S(1)}, u32[]{:S(2)}, u32[]{:S(2)}) collective-permute-start(bf16[2,96,256]{2,1,0:T(8,128)(2,1)S(1)} %pad_maximum_fusion), channel_id=1, source_target_pairs={{0,64},{64,0},{128,192},{192,128},{1,65},{65,1},{129,193},{193,129... | collective-permute-start | bytes 294920 | tf_op jit(solution)/shard_map/ppermute | solution.py:170
  27.2 4.2 %collective-permute-start.4 = (bf16[8,96,256]{2,1,0:T(8,128)(2,1)S(1)}, bf16[8,96,256]{2,1,0:T(8,128)(2,1)S(1)}, u32[]{:S(2)}, u32[]{:S(2)}) collective-permute-start(bf16[8,96,256]{2,1,0:T(8,128)(2,1)S(1)} %constant_dynamic-update-slice_fusion.near_ref), channel_id=1, source_target_pairs={{0,16},{16,0},{1,17},{17,1},{2,18},{18,2},{3,19},{19,3},{4,20},{20... | collective-permute-start | bytes 1179656 | tf_op jit(solution)/shard_map/ppermute | solution.py:171
  36.4 0.7 copy-start.1

commit v3 on v1

v3 whole, which is shorter than its diff:
```python
import functools
import math

import jax
import jax.numpy as jnp
from jax import lax
from jax.experimental import pallas as pl
from jax.experimental.pallas import tpu as pltpu
from jax.sharding import Mesh
from jax.sharding import PartitionSpec as P

EPSILON = 0.1
AXES = ("x", "yl", "k", "yh", "z")
ROW = ("x", "yl", "yh")
COL = ("k", "z")
DELTAS = (0, 1, -1, 4, 2, 3, -2, -3)
LANES = 128
TILE = 256
ROWS = 384
EXTRA = 8
LOG2E = math.log2(math.e)
SCALE = LOG2E / EPSILON
VMEM = pl.BlockSpec(memory_space=pltpu.VMEM)
HBM = pl.BlockSpec(memory_space=pltpu.HBM)
SMEM = pl.BlockSpec(memory_space=pltpu.SMEM)
PARAMS = pltpu.CompilerParams(vmem_limit_bytes=40 * 2**20)


def lane_pieces(length):
    return [slice(n, n + LANES) for n in range(0, length, LANES)]


def store_columns(pieces, columns_ref):
    for n, piece in enumerate(pieces):
        columns_ref[n * LANES : (n + 1) * LANES, :] = jnp.broadcast_to(piece, (LANES, LANES)).T


def repeated(column, length):
    return jnp.concatenate([column] * (length // LANES), axis=1)


def row_of_sums(partial):
    return jnp.sum(partial.T, axis=0, keepdims=True)


def from_z(array, delta):
    return lax.ppermute(array, "z", [(z, (z - delta) % 8) for z in range(8)])


def three_parts(row):
    high = row.astype(jnp.bfloat16).astype(jnp.float32)
    middle = (row - high).astype(jnp.bfloat16).astype(jnp.float32)
    return [high, middle, row - high - middle]


def copies_kernel(total, points_ref, mass_ref, send_ref, block_ref, held, held_mass, read, written):
    own, width = points_ref.shape
    reads = [pltpu.make_async_copy(points_ref, held, read.at[0]), pltpu.make_async_copy(mass_ref, held_mass, read.at[1])]
    for copy in reads:
        copy.start()
    for copy in reads:
        copy.wait()
    copies = [pltpu.make_async_copy(held, send_ref.at[d], written.at[d]) for d in range(send_ref.shape[0])]
    for copy in copies:
        copy.start()
    mass = held_mass[...]
    wide = held[...].astype(jnp.float32)
    halves = [wide[:, :LANES], wide[:, LANES:]]
    squares = halves[0] * halves[0] + halves[1] * halves[1]
    squares = jnp.concatenate([squares, jnp.zeros((LANES - own, LANES), jnp.float32)], axis=0)
    squares = row_of_sums(squares)[:, :own]
    base = LOG2E * jnp.log(mass * (1.0 / total)) - (0.5 * SCALE) * squares
    rows = three_parts(base) + three_parts(mass)
    rows.append(jnp.zeros((EXTRA - len(rows), own), jnp.float32))
    rows = jnp.concatenate(rows, axis=0)
    rows = jnp.concatenate([rows, jnp.zeros((EXTRA, LANES - own), jnp.float32)], axis=1)
    block_ref[...] = jnp.concatenate(halves + [rows], axis=0).astype(jnp.bfloat16)
    for copy in copies:
        copy.wait()


def right_kernel(rank_ref, near_ref, far_ref, right_ref, columns_ref, mass_ref):
    own = right_ref.shape[1]
    rank = rank_ref[1]
    for core, ref in enumerate((near_ref, far_ref)):
        for n, delta in enumerate(DELTAS):
            place = ((rank & 8) ^ (8 * core)) + ((rank + delta) & 7)
            right_ref[place, :, :LANES] = ref[n, :own, :]
            right_ref[place, :, LANES:] = ref[n, own : 2 * own, :]
            extra = ref[n].astype(jnp.float32)[2 * own :]
            base = jnp.sum(extra[0:3], axis=0, keepdims=True)
            columns_ref[place] = jnp.broadcast_to(base, (LANES, LANES)).T[:own]
    extra = near_ref[0].astype(jnp.float32)[2 * own :]
    mass_ref[...] = jnp.sum(extra[3:6], axis=0, keepdims=True)


def build_kernel(right_ref, columns_ref, mass_ref, left_ref, kernel_ref, send_ref):
    groups, own, width = left_ref.shape
    length = groups * own
    right = right_ref.reshape(length, width)
    columns = columns_ref.reshape(length, LANES)
    left = left_ref.reshape(length, width)
    sums = []
    for tile in range(0, length, TILE):
        squares = []
        for piece in range(tile, tile + TILE, LANES):
            wide = left[piece : piece + LANES, :].astype(jnp.float32)
            squares.append(row_of_sums(wide[:, :LANES] * wide[:, :LANES] + wide[:, LANES:] * wide[:, LANES:]))
        left_squares = (-0.5 * SCALE) * jnp.concatenate(squares, axis=1)
        total = jnp.zeros((8, TILE), jnp.float32)
        for start in range(0, length, ROWS):
            rows = slice(start, start + ROWS)
            inner = lax.dot_general(
                right[rows, :], left[tile : tile + TILE, :], (((1,), (1,)), ((), ())), preferred_element_type=jnp.float32
            )
            entries = jnp.exp2((SCALE * inner + left_squares) + repeated(columns[rows, :], TILE))
            kernel_ref[rows, tile : tile + TILE] = entries
            total = total + jnp.sum(entries.reshape(ROWS // 8, 8, TILE), axis=0)
        sums.append(jnp.sum(total, axis=0, keepdims=True))
    pieces = [total[:, piece] for total in sums for piece in lane_pieces(TILE)]
    send = jnp.concatenate(pieces + [mass_ref[...]], axis=1)
    for d in range(groups):
        send_ref[d] = send


def last_rows(got_ref, length, own):
    return jnp.concatenate([got_ref[d, :, length : length + own] for d in range(got_ref.shape[0])], axis=1)


def as_rows(row):
    return jnp.concatenate([row[:, piece] for piece in lane_pieces(row.shape[1])], axis=0)


def own_piece(flat_ref, rank, own):
    start = rank * own
    row, lane = start // LANES, start % LANES
    shift = (LANES - lane) % LANES
    first = pltpu.roll(jnp.broadcast_to(flat_ref[pl.ds(row, 1), :], (8, LANES)), shift, 1)
    second = pltpu.roll(jnp.broadcast_to(flat_ref[pl.ds(row + 1, 1), :], (8, LANES)), shift, 1)
    lanes = lax.broadcasted_iota(jnp.int32, (8, LANES), 1)
    return jnp.where(lanes < LANES - lane, first, second)[0:1]


def row_sums_kernel(total, own, rank_ref, kernel_ref, got_ref, send_ref, partial, flat):
    groups = got_ref.shape[0]
    length = groups * own
    count = length // LANES
    potential = -0.5 * jnp.log(as_rows(jnp.sum(got_ref[:, :, :length], axis=0)))
    flat[:count, :] = potential
    flat[count:, :] = jnp.zeros((flat.shape[0] - count, LANES), jnp.float32)
    growth = jnp.exp(potential)
    mass = last_rows(got_ref, length, own) * (1.0 / total)
    weight = jnp.concatenate([growth[n : n + 1] * mass[:, piece] for n, piece in enumerate(lane_pieces(length))], axis=1)

    def step(n, carry):
        rows = pl.ds(pl.multiple_of(n * 256, 256), 256)
        weighted = kernel_ref[rows, :] * weight
        partial[rows, :] = sum(weighted[:, piece] for piece in lane_pieces(length))
        return carry

    lax.fori_loop(0, length // 256, step, 0)
    own_mass = got_ref[rank_ref[0], :, length:] * (1.0 / total)
    mine = own_piece(flat, rank_ref[0], own) + jnp.log(own_mass)
    pieces = [row_of_sums(partial[piece, :]) for piece in lane_pieces(length)]
    send = jnp.concatenate(pieces + [mine], axis=1)
    for d in range(groups):
        send_ref[d] = send


def column_sums_kernel(own, rank_ref, kernel_ref, got_ref, send_ref, mine_ref, columns, flat):
    groups = got_ref.shape[0]
    length = groups * own
    count = length // LANES
    logs = jnp.log(as_rows(jnp.sum(got_ref[:, :, :length], axis=0)))
    before = as_rows(last_rows(got_ref, length, own))
    potential = 0.5 * (before - logs)
    flat[:count, :] = potential
    flat[count:, :] = jnp.zeros((flat.shape[0] - count, LANES), jnp.float32)
    growth = jnp.exp(potential)
    store_columns([growth[n : n + 1] for n in range(count)], columns)

    def step(n, sums):
        rows = pl.ds(pl.multiple_of(n * 16, 16), 16)
        weighted = kernel_ref[rows, :] * repeated(columns[rows, :], length)
        return sums + (weighted[:8] + weighted[8:])

    sums = lax.fori_loop(0, length // 16, step, jnp.zeros((8, length), jnp.float32), unroll=4)
    sums = jnp.sum(sums, axis=0, keepdims=True)
    for d in range(groups):
        send_ref[d] = sums[:, d * own : (d + 1) * own]
    mine_ref[...] = own_piece(flat, rank_ref[1], own)[:, :own]


def shards(points, mass):
    own, width = points.shape
    groups = 16
    length = groups * own
    total = length * groups
    f32 = jnp.float32
    ranks = jnp.stack([lax.axis_index(ROW), lax.axis_index(COL)]).astype(jnp.int32)
    send, block = pl.pallas_call(
        functools.partial(copies_kernel, total),
        out_shape=[
            jax.ShapeDtypeStruct((groups, own, width), points.dtype),
            jax.ShapeDtypeStruct((2 * own + EXTRA, LANES), points.dtype),
        ],
        in_specs=[HBM, HBM],
        out_specs=[HBM, VMEM],
        scratch_shapes=[
            pltpu.VMEM((own, width), points.dtype),
            pltpu.VMEM((1, own), f32),
            pltpu.SemaphoreType.DMA((2,)),
            pltpu.SemaphoreType.DMA((groups,)),
        ],
        compiler_params=PARAMS,
    )(points, mass.reshape(1, own))
    left = lax.all_to_all(send, ROW, 0, 0)
    above, below, across = from_z(block, 1), from_z(block, -1), from_z(block, 4)
    near = [jnp.stack([block, above, below, across])]
    near += [from_z(jnp.stack([block, above]), 2), from_z(jnp.stack([block, below]), -2)]
    near = jnp.concatenate(near)
    far = lax.ppermute(near, "k", [(0, 1), (1, 0)])
    right, columns, own_mass = pl.pallas_call(
        right_kernel,
        out_shape=[
            jax.ShapeDtypeStruct((groups, own, width), points.dtype),
            jax.ShapeDtypeStruct((groups, own, LANES), f32),
            jax.ShapeDtypeStruct((1, LANES), f32),
        ],
        in_specs=[SMEM, VMEM, VMEM],
        out_specs=[VMEM, VMEM, VMEM],
        compiler_params=PARAMS,
    )(ranks, near, far)
    message = jax.ShapeDtypeStruct((groups, 1, length + LANES), f32)
    kernel, send = pl.pallas_call(
        build_kernel,
        out_shape=[jax.ShapeDtypeStruct((length, length), f32), message],
        in_specs=[VMEM] * 4,
        out_specs=[VMEM, VMEM],
        compiler_params=PARAMS,
    )(right, columns, own_mass, left)
    got = lax.all_to_all(send, ROW, 0, 0)
    send = pl.pallas_call(
        functools.partial(row_sums_kernel, total, own),
        out_shape=message,
        in_specs=[SMEM, VMEM, VMEM],
        out_specs=VMEM,
        scratch_shapes=[pltpu.VMEM((length, LANES), f32), pltpu.VMEM((16, LANES), f32)],
        compiler_params=PARAMS,
    )(ranks, kernel, got)
    got = lax.all_to_all(send, COL, 0, 0)
    send, mine = pl.pallas_call(
        functools.partial(column_sums_kernel, own),
        out_shape=[jax.ShapeDtypeStruct((groups, 1, own), f32), jax.ShapeDtypeStruct((1, own), f32)],
        in_specs=[SMEM, VMEM, VMEM],
        out_specs=[VMEM, VMEM],
        scratch_shapes=[pltpu.VMEM((length, LANES), f32), pltpu.VMEM((16, LANES), f32)],
        compiler_params=PARAMS,
    )(ranks, kernel, got)
    sums = jnp.sum(lax.all_to_all(send, ROW, 0, 0), axis=0)
    return (0.5 * (mine - jnp.log(sums))).reshape(own)


def solution(mesh):
    fine = Mesh(mesh.devices.reshape(4, 2, 2, 2, 8), AXES)
    return jax.shard_map(
        shards,
        mesh=fine,
        in_specs=(P(AXES, None), P(AXES)),
        out_specs=P(AXES),
        check_vma=False,
    )
```

time: 104 us -> 75.7 us (0.73)
  waiting for transfers between devices: 34.6 us -> 3.91 us
  blocking collectives: 17.7 us -> 37 us
  other arithmetic: 11.7 us -> 0.65 us
  Pallas kernels: 0 us -> 7.57 us
  starting transfers between devices: 29.8 us -> 24.1 us
  matrix products: 5.1 us -> 0 us
  local copies, waits for them, and re-layouts: 4.52 us -> 1.52 us
    all_to_all x4 -> x1, waiting for transfers between devices: 34.6 us -> 0.48 us  [shards(): left = lax.all_to_all(send, ROW, 0, 0)]
    all_to_all x1 -> x3, blocking collectives: 13.5 us -> 37 us  [the longest x1 14.7 us: shards(): got = lax.all_to_all(send, COL, 0, 0)]
    all_to_all x4 -> x1, starting transfers between devices: 29.8 us -> 6.75 us  [shards(): left = lax.all_to_all(send, ROW, 0, 0)]
    ppermute x0 -> x6, starting transfers between devices: none -> 17.3 us  [the longest x5 14.1 us: from_z(): return lax.ppermute(array, 'z', [(z, (z - delta) % 8) for z in range(8)])]
    reduce_sum x8 -> x1, other arithmetic: 9.53 us -> 0.04 us  [shards(): sums = jnp.sum(lax.all_to_all(send, ROW, 0, 0), axis=0)]
    pallas_call x0 -> x5, Pallas kernels: none -> 7.57 us  [the longest x1 2.2 us: shards(): pl.pallas_call(build_kernel, out_shape=[jax.ShapeDtypeStruct((length, len...]
    dot_general x1 -> x0, matrix products: 5.1 us -> none  [shards(): lax.dot_general(right, left, (((1,), (1,)), ((), ())), preferred_element_...]
    all_gather x1 -> x0, blocking collectives: 4.22 us -> none  [shards(): left = lax.all_gather(left, 'k', axis=1).reshape(n_row * own, width)]
  transfers between devices with their start and end apart: 4 -> 7, of which waited for: 4 -> 4; matrix products, arithmetic and copies ran while one was open for 2% -> 0% of each run, Pallas kernels for 0% -> 1%
where the time goes in v3:
time: 75.7 us; the launch traced here: 74.9 us
  blocking collectives  37 us (49%)
  starting transfers between devices  24.1 us (32%)
  Pallas kernels  7.57 us (10%)
  waiting for transfers between devices  3.91 us (5%)
  local copies, waits for them, and re-layouts  1.52 us (2%)
    all_to_all x1, blocking collectives, shards(): got = lax.all_to_all(send, COL, 0, 0)  14.7 us
    ppermute x5, starting transfers between devices, from_z(): return lax.ppermute(array, 'z', [(z, (z - delta) % 8) for z in range(8)])  14.1 us
    all_to_all x1, blocking collectives, shards(): got = lax.all_to_all(send, ROW, 0, 0)  13.1 us
    all_to_all x1, blocking collectives, shards(): sums = jnp.sum(lax.all_to_all(send, ROW, 0, 0), axis=0)  9.19 us
    all_to_all x1, starting transfers between devices, shards(): left = lax.all_to_all(send, ROW, 0, 0)  6.75 us
    ppermute x1, starting transfers between devices, shards(): far = lax.ppermute(near, 'k', [(0, 1), (1, 0)])  3.2 us
    pallas_call x1, Pallas kernels, shards(): pl.pallas_call(build_kernel, out_shape=[jax.ShapeDtypeStruct((length, len...  2.2 us
    ppermute x5, waiting for transfers between devices, from_z(): return lax.ppermute(array, 'z', [(z, (z - delta) % 8) for z in range(8)])  2.13 us
  transfers between devices with their start and end apart: 7, of which 4 were waited for; matrix products, arithmetic and copies ran while one was open for 0% of the time, Pallas kernels for 1%

profile of v3, /device:TPU:1, one launch (start us, length us, event | category | flops | bytes accessed | tf_op | source)
XLA Modules:
  0.0 74.9 jit_solution(7589622808640595921)
XLA Ops:
  0.0 0.0 copy-start
  0.0 0.8 %copy-done = bf16[96,256]{1,0:T(8,128)(2,1)S(1)} copy-done((bf16[96,256]{1,0:T(8,128)(2,1)S(1)}, bf16[96,256]{1,0:T(8,128)(2,1)}, u32[]{:S(2)}) %copy-start) | copy-done | bytes 49176
  0.8 0.0 copy-start.1
  0.8 0.7 copy-done.1
  1.5 1.1 %shard_map.28 = (bf16[16,96,256]{2,1,0:T(8,128)(2,1)}, bf16[200,128]{1,0:T(8,128)(2,1)S(1)}) custom-call(bf16[96,256]{1,0:T(8,128)(2,1)S(1)} %copy-done, f32[1,96]{1,0:T(1,128)S(1)} %bitcast.20), custom_call_target="tpu_custom_call" | custom-call | tf_op jit(solution)/shard_map/pallas_call | solution.py:201
  2.5 7.8 %collective-permute-start.2 = (bf16[200,128]{1,0:T(8,128)(2,1)S(1)}, bf16[200,128]{1,0:T(8,128)(2,1)S(1)}, u32[]{:S(2)}, u32[]{:S(2)}) collective-permute-start(bf16[200,128]{1,0:T(8,128)(2,1)S(1)} %get-tuple-element.14), channel_id=1, source_target_pairs={{0,4},{1,5},{2,6},{3,7},{4,0},{5,1},{6,2},{7,3},{8,12},{9,13},{10,... | collective-permute-start | bytes 153608 | tf_op jit(solution)/shard_map/ppermute | solution.py:47
  10.4 0.7 collective-permute-start.1
  11.1 1.9 %collective-permute-start = (bf16[200,128]{1,0:T(8,128)(2,1)S(1)}, bf16[200,128]{1,0:T(8,128)(2,1)S(1)}, u32[]{:S(2)}, u32[]{:S(2)}) collective-permute-start(bf16[200,128]{1,0:T(8,128)(2,1)S(1)} %get-tuple-element.14), channel_id=1, source_target_pairs={{0,7},{1,0},{2,1},{3,2},{4,3},{5,4},{6,5},{7,6},{8,15},{9,8},{10,9... | collective-permute-start | bytes 153608 | tf_op jit(solution)/shard_map/ppermute | solution.py:47
  13.0 6.8 %all-to-all-start = ((bf16[16,96,256]{2,1,0:T(8,128)(2,1)}), bf16[16,96,256]{2,1,0:T(8,128)(2,1)S(1)}, u32[]{:S(2)}, u32[]{:S(2)}) async-start(bf16[16,96,256]{2,1,0:T(8,128)(2,1)} %get-tuple-element.18), calls=%async_computation | async-start | bytes 1572864 | tf_op jit(solution)/shard_map/all_to_all | solution.py:217
  19.8 0.0 collective-permute-done.1
  19.8 0.0 collective-permute-done
  19.9 0.1 collective-permute-start.4
  20.0 3.6 %collective-permute-start.3 = (bf16[2,200,128]{2,1,0:T(8,128)(2,1)S(1)}, bf16[2,200,128]{2,1,0:T(8,128)(2,1)S(1)}, u32[]{:S(2)}, u32[]{:S(2)}) collective-permute-start(bf16[2,200,128]{2,1,0:T(8,128)(2,1)S(1)} %get-tuple-element.24), channel_id=1, source_target_pairs={{0,6},{1,7},{2,0},{3,1},{4,2},{5,3},{6,4},{7,5},{8,14},{9,15},{10,... | collective-permute-start | bytes 307208 | tf_op jit(solution)/shard_map/ppermute | solution.py:47
  23.6 0.0 collective-permute-done.2
  23.6 2.1 %collective-permute-done.3 = bf16[2,200,128]{2,1,0:T(8,128)(2,1)S(1)} collective-permute-done((bf16[2,200,128]{2,1,0:T(8,128)(2,1)S(1)}, bf16[2,200,128]{2,1,0:T(8,128)(2,1)S(1)}, u32[]{:S(2)}, u32[]{:S(2)}) %collective-permute-start.3) | collective-permute-done | bytes 102432 | tf_op jit(solution)/shard_map/ppermute | solution.py:47
  25.7 0.1 collective-permute-done.4
  25.7 3.2 %collective-permute-start.5 = (bf16[8,200,128]{2,1,0:T(8,128)(2,1)S(1)}, bf16[8,200,128]{2,1,0:T(8,128)(2,1)S(1)}, u32[]{:S(2)}, u32[]{:S(2)}) collective-permute-start(bf16[8,200,128]{2,1,0:T(8,128)(2,1)S(1)} %constant_dynamic-update-slice_fusion.near_ref), channel_id=1, source_target_pairs={{0,16},{16,0},{1,17},{17,1},{2,18},{18,2},{3,19},{19,3},{4,20},{20... | collective-permute-start | bytes 1228808 | tf_op jit(solution)/shard_map/ppermute | solution.py:222
  28.9 0.1 pad_add_fusion.rank_ref
  29.0 1.3 %collective-permute-done.5.far_ref = bf16[8,200,128]{2,1,0:T(8,128)(2,1)S(1)} collective-permute-done((bf16[8,200,128]{2,1,0:T(8,128)(2,1)S(1)}, bf16[8,200,128]{2,1,0:T(8,128)(2,1)S(1)}, u32[]{:S(2)}, u32[]{:S(2)}) %collective-permute-start.5) | collective-permute-done | bytes 409632 | tf_op jit(solution)/shard_map/ppermute | solution.py:222
  30.3 1.0 %shard_map.29 = (bf16[16,96,256]{2,1,0:T(8,128)(2,1)S(1)}, f32[16,96,128]{2,1,0:T(8,128)S(1)}, f32[1,128]{1,0:T(1,128)S(1)}) custom-call(s32[2]{0:T(128)S(1)} %pad_add_fusion.rank_ref, bf16[8,200,128]{2,1,0:T(8,128)(2,1)S(1)} %constant_dynamic-update-slice_fusion.near_ref, bf16[8,200,128]{2,1,0:T(8,128)(2,1)S(1)} %collective-permute-done.5.far_ref), custom_call_target="tpu_custom_call" | custom-call | tf_op jit(solution)/shard_map/pallas_call | solution.py:223
  31.3 0.5 all-to-all-done.left_ref
  31.8 2.2 %shard_map.30 = (f32[1536,1536]{1,0:T(8,128)S(1)}, f32[16,1,1664]{2,1,0:T(1,128)S(1)}) custom-call(bf16[16,96,256]{2,1,0:T(8,128)(2,1)S(1)} %get-tuple-element.15.right_ref, f32[16,96,128]{2,1,0:T(8,128)S(1)} %get-tuple-element.16.columns_ref, f32[1,128]{1,0:T(1,128)S(1)} %get-tuple-element.17.mass_ref, bf16[16,96,256]{2,1,0:T(8,128)(2,1)S(1)} %all-to-all-done.left_ref), custom_call_target="tpu_custom_call" | custom-call | tf_op jit(solution)/shard_map/pallas_call | solution.py:235
  34.0 13.1 %all_to_all.20.got_ref = f32[16,1,1664]{2,1,0:T(1,128)S(1)} all-to-all(f32[16,1,1664]{2,1,0:T(1,128)S(1)} %get-tuple-element.20), channel_id=1, replica_groups=mesh['x'=4,'yl'=2,'k'=2,'yh'=2,'z'=8] {'x','yl','yh'}, dimensions={0} | all-to-all | bytes 212992 | tf_op jit(solution)/shard_map/all_to_all | solution.py:242
  47.1 1.6 %shard_map.31 = f32[16,1,1664]{2,1,0:T(1,128)S(1)} custom-call(s32[2]{0:T(128)S(1)} %pad_add_fusion.rank_ref, f32[1536,1536]{1,0:T(8,128)S(1)} %get-tuple-element.19.kernel_ref, f32[16,1,1664]{2,1,0:T(1,128)S(1)} %all_to_all.20.got_ref), custom_call_target="tpu_custom_call" | custom-call | tf_op jit(solution)/shard_map/pallas_call | solution.py:243
  48.7 14.7 %all_to_all.21.got_ref = f32[16,1,1664]{2,1,0:T(1,128)S(1)} all-to-all(f32[16,1,1664]{2,1,0:T(1,128)S(1)} %shard_map.31), channel_id=1, replica_groups=mesh['x'=4,'yl'=2,'k'=2,'yh'=2,'z'=8] {'k','z'}, dimensions={0} | all-to-all | bytes 212992 | tf_op jit(solution)/shard_map/all_to_all | solution.py:251
  63.4 1.7 %shard_map.32 = (f32[16,1,96]{2,1,0:T(1,128)S(1)}, f32[1,96]{1,0:T(1,128)S(1)}) custom-call(s32[2]{0:T(128)S(1)} %pad_add_fusion.rank_ref, f32[1536,1536]{1,0:T(8,128)S(1)} %get-tuple-element.19.kernel_ref, f32[16,1,1664]{2,1,0:T(1,128)S(1)} %all_to_all.21.got_ref), custom_call_target="tpu_custom_call" | custom-call | tf_op jit(solution)/shard_map/pallas_call | solution.py:252
  65.1 9.2 %all_to_all.22 = f32[16,1,96]{2,1,0:T(1,128)S(1)} all-to-all(f32[16,1,96]{2,1,0:T(1,128)S(1)} %get-tuple-element.22), channel_id=1, replica_groups=mesh['x'=4,'yl'=2,'k'=2,'yh'=2,'z'=8] {'x','yl','yh'}, dimensions={0} | all-to-all | bytes 12288 | tf_op jit(solution)/shard_map/all_to_all | solution.py:260
  74.3 0.5 fusion.1
  (8 shorter events, 0.1 us)
Async XLA Ops:
  0.0 0.8 %copy-start = (bf16[96,256]{1,0:T(8,128)(2,1)S(1)}, bf16[96,256]{1,0:T(8,128)(2,1)}, u32[]{:S(2)}) copy-start(bf16[96,256]{1,0:T(8,128)(2,1)} %points_ref.1) | copy-start | bytes 147460
  0.8 0.7 copy-start.1
  2.5 21.0 %collective-permute-start.2 = (bf16[200,128]{1,0:T(8,128)(2,1)S(1)}, bf16[200,128]{1,0:T(8,128)(2,1)S(1)}, u32[]{:S(2)}, u32[]{:S(2)}) collective-permute-start(bf16[200,128]{1,0:T(8,128)(2,1)S(1)} %get-tuple-element.14), channel_id=1, source_target_pairs={{0,4},{1,5},{2,6},{3,7},{4,0},{5,1},{6,2},{7,3},{8,12},{9,13},{10,... | collective-permute-start | bytes 153608 | tf_op jit(solution)/shard_map/ppermute | solution.py:47
  10.4 9.5 %collective-permute-start.1 = (bf16[200,128]{1,0:T(8,128)(2,1)S(1)}, bf16[200,128]{1,0:T(8,128)(2,1)S(1)}, u32[]{:S(2)}, u32[]{:S(2)}) collective-permute-start(bf16[200,128]{1,0:T(8,128)(2,1)S(1)} %get-tuple-element.14), channel_id=1, source_target_pairs={{0,1},{1,2},{2,3},{3,4},{4,5},{5,6},{6,7},{7,0},{8,9},{9,10},{10,1... | collective-permute-start | bytes 153608 | tf_op jit(solution)/shard_map/ppermute | solution.py:47
  11.1 8.7 %collective-permute-start = (bf16[200,128]{1,0:T(8,128)(2,1)S(1)}, bf16[200,128]{1,0:T(8,128)(2,1)S(1)}, u32[]{:S(2)}, u32[]{:S(2)}) collective-permute-start(bf16[200,128]{1,0:T(8,128)(2,1)S(1)} %get-tuple-element.14), channel_id=1, source_target_pairs={{0,7},{1,0},{2,1},{3,2},{4,3},{5,4},{6,5},{7,6},{8,15},{9,8},{10,9... | collective-permute-start | bytes 153608 | tf_op jit(solution)/shard_map/ppermute | solution.py:47
  13.0 18.7 %all-to-all-start = ((bf16[16,96,256]{2,1,0:T(8,128)(2,1)}), bf16[16,96,256]{2,1,0:T(8,128)(2,1)S(1)}, u32[]{:S(2)}, u32[]{:S(2)}) async-start(bf16[16,96,256]{2,1,0:T(8,128)(2,1)} %get-tuple-element.18), calls=%async_computation | async-start | bytes 1572864 | tf_op jit(solution)/shard_map/all_to_all | solution.py:217
  19.9 5.9 %collective-permute-start.4 = (bf16[2,200,128]{2,1,0:T(8,128)(2,1)S(1)}, bf16[2,200,128]{2,1,0:T(8,128)(2,1)S(1)}, u32[]{:S(2)}, u32[]{:S(2)}) collective-permute-start(bf16[2,200,128]{2,1,0:T(8,128)(2,1)S(1)} %get-tuple-element.23), channel_id=1, source_target_pairs={{0,2},{1,3},{2,4},{3,5},{4,6},{5,7},{6,0},{7,1},{8,10},{9,11},{10,... | collective-permute-start | bytes 307208 | tf_op jit(solution)/shard_map/ppermute | solution.py:47
  20.0 5.7 %collective-permute-start.3 = (bf16[2,200,128]{2,1,0:T(8,128)(2,1)S(1)}, bf16[2,200,128]{2,1,0:T(8,128)(2,1)S(1)}, u32[]{:S(2)}, u32[]{:S(2)}) collective-permute-start(bf16[2,200,128]{2,1,0:T(8,128)(2,1)S(1)} %get-tuple-element.24), channel_id=1, source_target_pairs={{0,6},{1,7},{2,0},{3,1},{4,2},{5,3},{6,4},{7,5},{8,14},{9,15},{10,... | collective-permute-start | bytes 307208 | tf_op jit(solution)/shard_map/ppermute | solution.py:47
  25.7 4.6 %collective-permute-start.5 = (bf16[8,200,128]{2,1,0:T(8,128)(2,1)S(1)}, bf16[8,200,128]{2,1,0:T(8,128)(2,1)S(1)}, u32[]{:S(2)}, u32[]{:S(2)}) collective-permute-start(bf16[8,200,128]{2,1,0:T(8,128)(2,1)S(1)} %constant_dynamic-update-slice_fusion.near_ref), channel_id=1, source_target_pairs={{0,16},{16,0},{1,17},{17,1},{2,18},{18,2},{3,19},{19,3},{4,20},{20... | collective-permute-start | bytes 1228808 | tf_op jit(solution)/shard_map/ppermute | solution.py:222

commit v4 on v3

--- a/solution.py
+++ b/solution.py
@@ -13,10 +13,10 @@
 AXES = ("x", "yl", "k", "yh", "z")
 ROW = ("x", "yl", "yh")
 COL = ("k", "z")
-DELTAS = (0, 1, -1, 4, 2, 3, -2, -3)
+SIDE = ((1, 0), (1, 1), (2, 0), (2, 1), (3, 0), (3, 1), (4, 0))
 LANES = 128
-TILE = 256
-ROWS = 384
+TILE = 512
+ROWS = 768
 EXTRA = 8
 LOG2E = math.log2(math.e)
 SCALE = LOG2E / EPSILON
@@ -43,8 +43,9 @@
     return jnp.sum(partial.T, axis=0, keepdims=True)
 
 
-def from_z(array, delta):
-    return lax.ppermute(array, "z", [(z, (z - delta) % 8) for z in range(8)])
+def along_z(array, step):
+    pairs = [(z, (z - step) % 8) for z in range(8)] + [(8 + z, 8 + (z + step) % 8) for z in range(8)]
+    return lax.ppermute(array, ("k", "z"), pairs)
 
 
 def three_parts(row):
@@ -79,19 +80,28 @@
         copy.wait()
 
 
-def right_kernel(rank_ref, near_ref, far_ref, right_ref, columns_ref, mass_ref):
+def place_blocks(blocks_ref, places, core, z, right_ref, columns_ref):
     own = right_ref.shape[1]
-    rank = rank_ref[1]
-    for core, ref in enumerate((near_ref, far_ref)):
-        for n, delta in enumerate(DELTAS):
-            place = ((rank & 8) ^ (8 * core)) + ((rank + delta) & 7)
-            right_ref[place, :, :LANES] = ref[n, :own, :]
-            right_ref[place, :, LANES:] = ref[n, own : 2 * own, :]
-            extra = ref[n].astype(jnp.float32)[2 * own :]
-            base = jnp.sum(extra[0:3], axis=0, keepdims=True)
-            columns_ref[place] = jnp.broadcast_to(base, (LANES, LANES)).T[:own]
-    extra = near_ref[0].astype(jnp.float32)[2 * own :]
+    for n, (distance, other) in enumerate(places):
+        place = 8 * (core ^ other) + ((z + (1 - 2 * core) * distance) & 7)
+        right_ref[place, :, :LANES] = blocks_ref[n, :own, :]
+        right_ref[place, :, LANES:] = blocks_ref[n, own : 2 * own, :]
+        extra = blocks_ref[n].astype(jnp.float32)[2 * own :]
+        base = jnp.sum(extra[0:3], axis=0, keepdims=True)
+        columns_ref[place] = jnp.broadcast_to(base, (LANES, LANES)).T[:own]
+
+
+def near_kernel(rank_ref, pair_ref, blocks_ref, right_ref, columns_ref, mass_ref):
+    core, z = rank_ref[1] // 8, rank_ref[1] % 8
+    place_blocks(pair_ref, ((0, 0), (0, 1)), core, z, right_ref, columns_ref)
+    place_blocks(blocks_ref, SIDE, core, z, right_ref, columns_ref)
+    extra = pair_ref[0].astype(jnp.float32)[2 * right_ref.shape[1] :]
     mass_ref[...] = jnp.sum(extra[3:6], axis=0, keepdims=True)
+
+
+def far_kernel(rank_ref, blocks_ref, half_right_ref, half_columns_ref, right_ref, columns_ref):
+    core, z = rank_ref[1] // 8, rank_ref[1] % 8
+    place_blocks(blocks_ref, SIDE, 1 - core, z, right_ref, columns_ref)
 
 
 def build_kernel(right_ref, columns_ref, mass_ref, left_ref, kernel_ref, send_ref):
@@ -213,24 +223,34 @@
             pltpu.SemaphoreType.DMA((groups,)),
         ],
         compiler_params=PARAMS,
-    )(points, mass.reshape(1, own))
+    )(*(pltpu.with_memory_space_constraint(a, pltpu.HBM) for a in (points, mass.reshape(1, own))))
     left = lax.all_to_all(send, ROW, 0, 0)
-    above, below, across = from_z(block, 1), from_z(block, -1), from_z(block, 4)
-    near = [jnp.stack([block, above, below, across])]
-    near += [from_z(jnp.stack([block, above]), 2), from_z(jnp.stack([block, below]), -2)]
-    near = jnp.concatenate(near)
-    far = lax.ppermute(near, "k", [(0, 1), (1, 0)])
+    swap = [(0, 1), (1, 0)]
+    pair = jnp.stack([block, lax.ppermute(block, "k", swap)])
+    first = along_z(pair, 1)
+    across = lax.ppermute(block, "z", [(z, z ^ 4) for z in range(8)])
+    pair, first, across = lax.optimization_barrier((pair, first, across))
+    side = jnp.concatenate([first, along_z(jnp.concatenate([pair, first]), 2), across[None]])
+    far = lax.ppermute(side, "k", swap)
+    ordered = [
+        jax.ShapeDtypeStruct((groups, own, width), points.dtype),
+        jax.ShapeDtypeStruct((groups, own, LANES), f32),
+    ]
     right, columns, own_mass = pl.pallas_call(
-        right_kernel,
-        out_shape=[
-            jax.ShapeDtypeStruct((groups, own, width), points.dtype),
-            jax.ShapeDtypeStruct((groups, own, LANES), f32),
-            jax.ShapeDtypeStruct((1, LANES), f32),
-        ],
+        near_kernel,
+        out_shape=ordered + [jax.ShapeDtypeStruct((1, LANES), f32)],
         in_specs=[SMEM, VMEM, VMEM],
         out_specs=[VMEM, VMEM, VMEM],
         compiler_params=PARAMS,
-    )(ranks, near, far)
+    )(ranks, pair, side)
+    right, columns = pl.pallas_call(
+        far_kernel,
+        out_shape=ordered,
+        in_specs=[SMEM, VMEM, VMEM, VMEM],
+        out_specs=[VMEM, VMEM],
+        input_output_aliases={2: 0, 3: 1},
+        compiler_params=PARAMS,
+    )(ranks, far, right, columns)
     message = jax.ShapeDtypeStruct((groups, 1, length + LANES), f32)
     kernel, send = pl.pallas_call(
         build_kernel,

time: 75.7 us -> 74 us (0.978)
  waiting for transfers between devices: 3.91 us -> 12.3 us
  starting transfers between devices: 24.1 us -> 17.7 us
  blocking collectives: 37 us -> 33.7 us
  local copies, waits for them, and re-layouts: 1.52 us -> 0 us
  Pallas kernels: 7.57 us -> 8.7 us
    ppermute x6 -> x5, starting transfers between devices: 17.3 us -> 10.9 us  [the longest x1 5.9 us: shards(): across = lax.ppermute(block, 'z', [(z, z ^ 4) for z in range(8)])]
    ppermute x6 -> x5, waiting for transfers between devices: 3.43 us -> 9.12 us  [the longest x2 7.72 us: along_z(): return lax.ppermute(array, ('k', 'z'), pairs)]
    all_to_all x1, waiting for transfers between devices: 0.48 us -> 3.17 us  [shards(): left = lax.all_to_all(send, ROW, 0, 0)]
    all_to_all x1, blocking collectives: 13.1 us -> 10.6 us  [shards(): got = lax.all_to_all(send, ROW, 0, 0)]
    unnamed x9 -> x0, local copies, waits for them, and re-layouts: 1.51 us -> none
    pallas_call x1, Pallas kernels: 1.08 us -> 1.84 us  [shards(): pl.pallas_call(functools.partial(copies_kernel, total), out_shape=[jax.Sh...]
    pallas_call x1 -> x2, Pallas kernels: 0.97 us -> 1.55 us  [the longest x1 0.82 us: shards(): pl.pallas_call(near_kernel, out_shape=ordered + [jax.ShapeDtypeStruct((1,...]
  transfers between devices with their start and end apart: 7 -> 6, of which waited for: 4 -> 4; matrix products, arithmetic and copies ran while one was open for 0% -> 0% of each run, Pallas kernels for 1% -> 2%
where the time goes in v4:
time: 74 us; the launch traced here: 73.2 us
  blocking collectives  33.7 us (46%)
  starting transfers between devices  17.7 us (24%)
  waiting for transfers between devices  12.3 us (17%)
  Pallas kernels  8.7 us (12%)
    all_to_all x1, blocking collectives, shards(): got = lax.all_to_all(send, COL, 0, 0)  14 us
    all_to_all x1, blocking collectives, shards(): got = lax.all_to_all(send, ROW, 0, 0)  10.6 us
    all_to_all x1, blocking collectives, shards(): sums = jnp.sum(lax.all_to_all(send, ROW, 0, 0), axis=0)  9.19 us
    ppermute x2, waiting for transfers between devices, along_z(): return lax.ppermute(array, ('k', 'z'), pairs)  7.72 us
    all_to_all x1, starting transfers between devices, shards(): left = lax.all_to_all(send, ROW, 0, 0)  6.75 us
    ppermute x1, starting transfers between devices, shards(): across = lax.ppermute(block, 'z', [(z, z ^ 4) for z in range(8)])  5.9 us
    ppermute x1, starting transfers between devices, shards(): pair = jnp.stack([block, lax.ppermute(block, 'k', swap)])  3.33 us
    all_to_all x1, waiting for transfers between devices, shards(): left = lax.all_to_all(send, ROW, 0, 0)  3.17 us
  transfers between devices with their start and end apart: 6, of which 4 were waited for; matrix products, arithmetic and copies ran while one was open for 0% of the time, Pallas kernels for 2%

profile of v4, /device:TPU:1, one launch (start us, length us, event | category | flops | bytes accessed | tf_op | source)
XLA Modules:
  0.0 73.2 jit_solution(847826260093770123)
XLA Ops:
  0.0 1.8 %shard_map.28 = (bf16[16,96,256]{2,1,0:T(8,128)(2,1)}, bf16[200,128]{1,0:T(8,128)(2,1)S(1)}) custom-call(bf16[96,256]{1,0:T(8,128)(2,1)} %points_ref.1, f32[1,96]{1,0:T(1,128)} %bitcast.17), custom_call_target="tpu_custom_call" | custom-call | tf_op jit(solution)/shard_map/pallas_call | solution.py:211
  1.8 3.3 %collective-permute-start = (bf16[200,128]{1,0:T(8,128)(2,1)S(1)}, bf16[200,128]{1,0:T(8,128)(2,1)S(1)}, u32[]{:S(2)}, u32[]{:S(2)}) collective-permute-start(bf16[200,128]{1,0:T(8,128)(2,1)S(1)} %get-tuple-element.19), channel_id=1, source_target_pairs={{0,16},{16,0},{1,17},{17,1},{2,18},{18,2},{3,19},{19,3},{4,20},{20... | collective-permute-start | bytes 153608 | tf_op jit(solution)/shard_map/ppermute | solution.py:229
  5.2 0.9 %collective-permute-done = bf16[200,128]{1,0:T(8,128)(2,1)S(1)} collective-permute-done((bf16[200,128]{1,0:T(8,128)(2,1)S(1)}, bf16[200,128]{1,0:T(8,128)(2,1)S(1)}, u32[]{:S(2)}, u32[]{:S(2)}) %collective-permute-start) | collective-permute-done | bytes 51232 | tf_op jit(solution)/shard_map/ppermute | solution.py:229
  6.1 0.1 collective-permute-start.1
  6.2 5.9 %collective-permute-start.2 = (bf16[200,128]{1,0:T(8,128)(2,1)S(1)}, bf16[200,128]{1,0:T(8,128)(2,1)S(1)}, u32[]{:S(2)}, u32[]{:S(2)}) collective-permute-start(bf16[200,128]{1,0:T(8,128)(2,1)S(1)} %get-tuple-element.19), channel_id=1, source_target_pairs={{0,4},{1,5},{2,6},{3,7},{4,0},{5,1},{6,2},{7,3},{8,12},{9,13},{10,... | collective-permute-start | bytes 153608 | tf_op jit(solution)/shard_map/ppermute | solution.py:231
  12.1 6.8 %all-to-all-start = ((bf16[16,96,256]{2,1,0:T(8,128)(2,1)}), bf16[16,96,256]{2,1,0:T(8,128)(2,1)S(1)}, u32[]{:S(2)}, u32[]{:S(2)}) async-start(bf16[16,96,256]{2,1,0:T(8,128)(2,1)} %get-tuple-element.28), calls=%async_computation | async-start | bytes 1572864 | tf_op jit(solution)/shard_map/all_to_all | solution.py:227
  18.8 0.0 collective-permute-done.2
  18.8 0.0 collective-permute-done.1
  18.9 1.3 %collective-permute-start.3 = (bf16[4,200,128]{2,1,0:T(8,128)(2,1)S(1)}, bf16[4,200,128]{2,1,0:T(8,128)(2,1)S(1)}, u32[]{:S(2)}, u32[]{:S(2)}) collective-permute-start(bf16[4,200,128]{2,1,0:T(8,128)(2,1)S(1)} %pad_maximum_fusion.1), channel_id=1, source_target_pairs={{0,6},{1,7},{2,0},{3,1},{4,2},{5,3},{6,4},{7,5},{16,18},{17,19},{1... | collective-permute-start | bytes 614408 | tf_op jit(solution)/shard_map/ppermute | solution.py:48
  20.1 7.7 %collective-permute-done.3 = bf16[4,200,128]{2,1,0:T(8,128)(2,1)S(1)} collective-permute-done((bf16[4,200,128]{2,1,0:T(8,128)(2,1)S(1)}, bf16[4,200,128]{2,1,0:T(8,128)(2,1)S(1)}, u32[]{:S(2)}, u32[]{:S(2)}) %collective-permute-start.3) | collective-permute-done | bytes 204832 | tf_op jit(solution)/shard_map/ppermute | solution.py:48
  27.9 0.4 collective-permute-start.4
  28.3 0.1 pad_add_fusion.rank_ref
  28.3 0.8 %shard_map.29 = (bf16[16,96,256]{2,1,0:T(8,128)(2,1)S(1)}, f32[16,96,128]{2,1,0:T(8,128)S(1)}, f32[1,128]{1,0:T(1,128)S(1)}) custom-call(s32[2]{0:T(128)S(1)} %pad_add_fusion.rank_ref, bf16[2,200,128]{2,1,0:T(8,128)(2,1)S(1)} %pad_maximum_fusion.2.pair_ref, bf16[7,200,128]{2,1,0:T(8,128)(2,1)S(1)} %pad_maximum_fusion.blocks_ref), custom_call_target="tpu_custom_call" | custom-call | tf_op jit(solution)/shard_map/pallas_call | solution.py:239
  29.2 0.5 collective-permute-done.4.blocks_ref
  29.7 0.7 shard_map.30
  30.4 3.2 %all-to-all-done.left_ref = bf16[16,96,256]{2,1,0:T(8,128)(2,1)S(1)} async-done(((bf16[16,96,256]{2,1,0:T(8,128)(2,1)}), bf16[16,96,256]{2,1,0:T(8,128)(2,1)S(1)}, u32[]{:S(2)}, u32[]{:S(2)}) %all-to-all-start) | async-done | bytes 786464 | tf_op jit(solution)/shard_map/all_to_all | solution.py:227
  33.6 2.0 %shard_map.31 = (f32[1536,1536]{1,0:T(8,128)S(1)}, f32[16,1,1664]{2,1,0:T(1,128)S(1)}) custom-call(bf16[16,96,256]{2,1,0:T(8,128)(2,1)S(1)} %get-tuple-element.25.right_ref, f32[16,96,128]{2,1,0:T(8,128)S(1)} %get-tuple-element.26.columns_ref, f32[1,128]{1,0:T(1,128)S(1)} %get-tuple-element.27.mass_ref, bf16[16,96,256]{2,1,0:T(8,128)(2,1)S(1)} %all-to-all-done.left_ref), custom_call_target="tpu_custom_call" | custom-call | tf_op jit(solution)/shard_map/pallas_call | solution.py:255
  35.6 10.6 %all_to_all.20.got_ref = f32[16,1,1664]{2,1,0:T(1,128)S(1)} all-to-all(f32[16,1,1664]{2,1,0:T(1,128)S(1)} %get-tuple-element.30), channel_id=1, replica_groups=mesh['x'=4,'yl'=2,'k'=2,'yh'=2,'z'=8] {'x','yl','yh'}, dimensions={0} | all-to-all | bytes 212992 | tf_op jit(solution)/shard_map/all_to_all | solution.py:262
  46.1 1.6 %shard_map.32 = f32[16,1,1664]{2,1,0:T(1,128)S(1)} custom-call(s32[2]{0:T(128)S(1)} %pad_add_fusion.rank_ref, f32[1536,1536]{1,0:T(8,128)S(1)} %get-tuple-element.29.kernel_ref, f32[16,1,1664]{2,1,0:T(1,128)S(1)} %all_to_all.20.got_ref), custom_call_target="tpu_custom_call" | custom-call | tf_op jit(solution)/shard_map/pallas_call | solution.py:263
  47.7 14.0 %all_to_all.21.got_ref = f32[16,1,1664]{2,1,0:T(1,128)S(1)} all-to-all(f32[16,1,1664]{2,1,0:T(1,128)S(1)} %shard_map.32), channel_id=1, replica_groups=mesh['x'=4,'yl'=2,'k'=2,'yh'=2,'z'=8] {'k','z'}, dimensions={0} | all-to-all | bytes 212992 | tf_op jit(solution)/shard_map/all_to_all | solution.py:271
  61.7 1.7 %shard_map.33 = (f32[16,1,96]{2,1,0:T(1,128)S(1)}, f32[1,96]{1,0:T(1,128)S(1)}) custom-call(s32[2]{0:T(128)S(1)} %pad_add_fusion.rank_ref, f32[1536,1536]{1,0:T(8,128)S(1)} %get-tuple-element.29.kernel_ref, f32[16,1,1664]{2,1,0:T(1,128)S(1)} %all_to_all.21.got_ref), custom_call_target="tpu_custom_call" | custom-call | tf_op jit(solution)/shard_map/pallas_call | solution.py:272
  63.4 9.2 %all_to_all.22 = f32[16,1,96]{2,1,0:T(1,128)S(1)} all-to-all(f32[16,1,96]{2,1,0:T(1,128)S(1)} %get-tuple-element.32), channel_id=1, replica_groups=mesh['x'=4,'yl'=2,'k'=2,'yh'=2,'z'=8] {'x','yl','yh'}, dimensions={0} | all-to-all | bytes 12288 | tf_op jit(solution)/shard_map/all_to_all | solution.py:280
  72.7 0.5 fusion.1
  (4 shorter events, 0.1 us)
Async XLA Ops:
  1.8 4.2 %collective-permute-start = (bf16[200,128]{1,0:T(8,128)(2,1)S(1)}, bf16[200,128]{1,0:T(8,128)(2,1)S(1)}, u32[]{:S(2)}, u32[]{:S(2)}) collective-permute-start(bf16[200,128]{1,0:T(8,128)(2,1)S(1)} %get-tuple-element.19), channel_id=1, source_target_pairs={{0,16},{16,0},{1,17},{17,1},{2,18},{18,2},{3,19},{19,3},{4,20},{20... | collective-permute-start | bytes 153608 | tf_op jit(solution)/shard_map/ppermute | solution.py:229
  6.1 12.8 %collective-permute-start.1 = (bf16[2,200,128]{2,1,0:T(8,128)(2,1)S(1)}, bf16[2,200,128]{2,1,0:T(8,128)(2,1)S(1)}, u32[]{:S(2)}, u32[]{:S(2)}) collective-permute-start(bf16[2,200,128]{2,1,0:T(8,128)(2,1)S(1)} %pad_maximum_fusion.2.pair_ref), channel_id=1, source_target_pairs={{0,7},{1,0},{2,1},{3,2},{4,3},{5,4},{6,5},{7,6},{16,17},{17,18},{1... | collective-permute-start | bytes 307208 | tf_op jit(solution)/shard_map/ppermute | solution.py:48
  6.2 12.7 %collective-permute-start.2 = (bf16[200,128]{1,0:T(8,128)(2,1)S(1)}, bf16[200,128]{1,0:T(8,128)(2,1)S(1)}, u32[]{:S(2)}, u32[]{:S(2)}) collective-permute-start(bf16[200,128]{1,0:T(8,128)(2,1)S(1)} %get-tuple-element.19), channel_id=1, source_target_pairs={{0,4},{1,5},{2,6},{3,7},{4,0},{5,1},{6,2},{7,3},{8,12},{9,13},{10,... | collective-permute-start | bytes 153608 | tf_op jit(solution)/shard_map/ppermute | solution.py:231
  12.1 21.5 %all-to-all-start = ((bf16[16,96,256]{2,1,0:T(8,128)(2,1)}), bf16[16,96,256]{2,1,0:T(8,128)(2,1)S(1)}, u32[]{:S(2)}, u32[]{:S(2)}) async-start(bf16[16,96,256]{2,1,0:T(8,128)(2,1)} %get-tuple-element.28), calls=%async_computation | async-start | bytes 1572864 | tf_op jit(solution)/shard_map/all_to_all | solution.py:227
  18.9 9.0 %collective-permute-start.3 = (bf16[4,200,128]{2,1,0:T(8,128)(2,1)S(1)}, bf16[4,200,128]{2,1,0:T(8,128)(2,1)S(1)}, u32[]{:S(2)}, u32[]{:S(2)}) collective-permute-start(bf16[4,200,128]{2,1,0:T(8,128)(2,1)S(1)} %pad_maximum_fusion.1), channel_id=1, source_target_pairs={{0,6},{1,7},{2,0},{3,1},{4,2},{5,3},{6,4},{7,5},{16,18},{17,19},{1... | collective-permute-start | bytes 614408 | tf_op jit(solution)/shard_map/ppermute | solution.py:48
  27.9 1.8 %collective-permute-start.4 = (bf16[7,200,128]{2,1,0:T(8,128)(2,1)S(1)}, bf16[7,200,128]{2,1,0:T(8,128)(2,1)S(1)}, u32[]{:S(2)}, u32[]{:S(2)}) collective-permute-start(bf16[7,200,128]{2,1,0:T(8,128)(2,1)S(1)} %pad_maximum_fusion.blocks_ref), channel_id=1, source_target_pairs={{0,16},{16,0},{1,17},{17,1},{2,18},{18,2},{3,19},{19,3},{4,20},{20... | collective-permute-start | bytes 1075208 | tf_op jit(solution)/shard_map/ppermute | solution.py:234

commit v5 on v4

--- a/solution.py
+++ b/solution.py
@@ -54,16 +54,13 @@
     return [high, middle, row - high - middle]
 
 
-def copies_kernel(total, points_ref, mass_ref, send_ref, block_ref, held, held_mass, read, written):
-    own, width = points_ref.shape
+def block_kernel(total, points_ref, mass_ref, block_ref, held, held_mass, read):
+    own = points_ref.shape[0]
     reads = [pltpu.make_async_copy(points_ref, held, read.at[0]), pltpu.make_async_copy(mass_ref, held_mass, read.at[1])]
     for copy in reads:
         copy.start()
     for copy in reads:
         copy.wait()
-    copies = [pltpu.make_async_copy(held, send_ref.at[d], written.at[d]) for d in range(send_ref.shape[0])]
-    for copy in copies:
-        copy.start()
     mass = held_mass[...]
     wide = held[...].astype(jnp.float32)
     halves = [wide[:, :LANES], wide[:, LANES:]]
@@ -76,6 +73,15 @@
     rows = jnp.concatenate(rows, axis=0)
     rows = jnp.concatenate([rows, jnp.zeros((EXTRA, LANES - own), jnp.float32)], axis=1)
     block_ref[...] = jnp.concatenate(halves + [rows], axis=0).astype(jnp.bfloat16)
+
+
+def copies_kernel(block_ref, send_ref, held, written):
+    own = held.shape[0]
+    held[:, :LANES] = block_ref[:own, :]
+    held[:, LANES:] = block_ref[own : 2 * own, :]
+    copies = [pltpu.make_async_copy(held, send_ref.at[d], written.at[d]) for d in range(send_ref.shape[0])]
+    for copy in copies:
+        copy.start()
     for copy in copies:
         copy.wait()
 
@@ -208,30 +214,35 @@
     total = length * groups
     f32 = jnp.float32
     ranks = jnp.stack([lax.axis_index(ROW), lax.axis_index(COL)]).astype(jnp.int32)
-    send, block = pl.pallas_call(
-        functools.partial(copies_kernel, total),
-        out_shape=[
-            jax.ShapeDtypeStruct((groups, own, width), points.dtype),
-            jax.ShapeDtypeStruct((2 * own + EXTRA, LANES), points.dtype),
-        ],
+    block = pl.pallas_call(
+        functools.partial(block_kernel, total),
+        out_shape=jax.ShapeDtypeStruct((2 * own + EXTRA, LANES), points.dtype),
         in_specs=[HBM, HBM],
-        out_specs=[HBM, VMEM],
+        out_specs=VMEM,
         scratch_shapes=[
             pltpu.VMEM((own, width), points.dtype),
             pltpu.VMEM((1, own), f32),
             pltpu.SemaphoreType.DMA((2,)),
-            pltpu.SemaphoreType.DMA((groups,)),
         ],
         compiler_params=PARAMS,
     )(*(pltpu.with_memory_space_constraint(a, pltpu.HBM) for a in (points, mass.reshape(1, own))))
-    left = lax.all_to_all(send, ROW, 0, 0)
+    send = pl.pallas_call(
+        copies_kernel,
+        out_shape=jax.ShapeDtypeStruct((groups, own, width), points.dtype),
+        in_specs=[VMEM],
+        out_specs=HBM,
+        scratch_shapes=[pltpu.VMEM((own, width), points.dtype), pltpu.SemaphoreType.DMA((groups,))],
+        compiler_params=PARAMS,
+    )(block)
     swap = [(0, 1), (1, 0)]
-    pair = jnp.stack([block, lax.ppermute(block, "k", swap)])
+    other, send = lax.optimization_barrier((lax.ppermute(block, "k", swap), send))
+    pair = jnp.stack([block, other])
     first = along_z(pair, 1)
     across = lax.ppermute(block, "z", [(z, z ^ 4) for z in range(8)])
     pair, first, across = lax.optimization_barrier((pair, first, across))
     side = jnp.concatenate([first, along_z(jnp.concatenate([pair, first]), 2), across[None]])
     far = lax.ppermute(side, "k", swap)
+    left = lax.all_to_all(send, ROW, 0, 0)
     ordered = [
         jax.ShapeDtypeStruct((groups, own, width), points.dtype),
         jax.ShapeDtypeStruct((groups, own, LANES), f32),

time: 74 us -> 73.1 us (0.988)
  waiting for transfers between devices: 12.3 us -> 11.5 us
    ppermute x1, waiting for transfers between devices: 0.88 us -> 0.01 us  [shards(): lax.ppermute(block, 'k', swap)]
    pallas_call x1 -> x2, Pallas kernels: 1.84 us -> 1.98 us  [the longest x1 1.04 us: shards(): pl.pallas_call(copies_kernel, out_shape=jax.ShapeDtypeStruct((groups, own...]
  transfers between devices with their start and end apart: 6 -> 6, of which waited for: 4 -> 3; matrix products, arithmetic and copies ran while one was open for 0% -> 0% of each run, Pallas kernels for 2% -> 4%
where the time goes in v5:
time: 73.1 us; the launch traced here: 72.3 us
  blocking collectives  33.4 us (46%)
  starting transfers between devices  17.7 us (24%)
  waiting for transfers between devices  11.5 us (16%)
  Pallas kernels  8.83 us (12%)
    all_to_all x1, blocking collectives, shards(): got = lax.all_to_all(send, COL, 0, 0)  13.6 us
    all_to_all x1, blocking collectives, shards(): got = lax.all_to_all(send, ROW, 0, 0)  10.6 us
    all_to_all x1, blocking collectives, shards(): sums = jnp.sum(lax.all_to_all(send, ROW, 0, 0), axis=0)  9.19 us
    ppermute x2, waiting for transfers between devices, along_z(): return lax.ppermute(array, ('k', 'z'), pairs)  7.72 us
    all_to_all x1, starting transfers between devices, shards(): left = lax.all_to_all(send, ROW, 0, 0)  6.75 us
    ppermute x1, starting transfers between devices, shards(): across = lax.ppermute(block, 'z', [(z, z ^ 4) for z in range(8)])  5.9 us
    all_to_all x1, waiting for transfers between devices, shards(): left = lax.all_to_all(send, ROW, 0, 0)  3.33 us
    ppermute x1, starting transfers between devices, shards(): lax.ppermute(block, 'k', swap)  3.33 us
  transfers between devices with their start and end apart: 6, of which 3 were waited for; matrix products, arithmetic and copies ran while one was open for 0% of the time, Pallas kernels for 4%

profile of v5, /device:TPU:1, one launch (start us, length us, event | category | flops | bytes accessed | tf_op | source)
XLA Modules:
  0.0 72.3 jit_solution(7631731292581565412)
XLA Ops:
  0.0 0.9 %shard_map.28.block_ref = bf16[200,128]{1,0:T(8,128)(2,1)S(1)} custom-call(bf16[96,256]{1,0:T(8,128)(2,1)} %points_ref.1, f32[1,96]{1,0:T(1,128)} %bitcast.17), custom_call_target="tpu_custom_call" | custom-call | tf_op jit(solution)/shard_map/pallas_call | solution.py:217
  0.9 3.3 %collective-permute-start = (bf16[200,128]{1,0:T(8,128)(2,1)S(1)}, bf16[200,128]{1,0:T(8,128)(2,1)S(1)}, u32[]{:S(2)}, u32[]{:S(2)}) collective-permute-start(bf16[200,128]{1,0:T(8,128)(2,1)S(1)} %shard_map.28.block_ref), channel_id=1, source_target_pairs={{0,16},{16,0},{1,17},{17,1},{2,18},{18,2},{3,19},{19,3},{4,20},{20... | collective-permute-start | bytes 153608 | tf_op jit(solution)/shard_map/ppermute | solution.py:238
  4.3 1.0 %shard_map.29 = bf16[16,96,256]{2,1,0:T(8,128)(2,1)} custom-call(bf16[200,128]{1,0:T(8,128)(2,1)S(1)} %shard_map.28.block_ref), custom_call_target="tpu_custom_call" | custom-call | tf_op jit(solution)/shard_map/pallas_call | solution.py:229
  5.3 0.0 collective-permute-done
  5.4 0.1 collective-permute-start.1
  5.4 5.9 %collective-permute-start.2 = (bf16[200,128]{1,0:T(8,128)(2,1)S(1)}, bf16[200,128]{1,0:T(8,128)(2,1)S(1)}, u32[]{:S(2)}, u32[]{:S(2)}) collective-permute-start(bf16[200,128]{1,0:T(8,128)(2,1)S(1)} %shard_map.28.block_ref), channel_id=1, source_target_pairs={{0,4},{1,5},{2,6},{3,7},{4,0},{5,1},{6,2},{7,3},{8,12},{9,13},{10,... | collective-permute-start | bytes 153608 | tf_op jit(solution)/shard_map/ppermute | solution.py:241
  11.3 6.8 %all-to-all-start = ((bf16[16,96,256]{2,1,0:T(8,128)(2,1)}), bf16[16,96,256]{2,1,0:T(8,128)(2,1)S(1)}, u32[]{:S(2)}, u32[]{:S(2)}) async-start(bf16[16,96,256]{2,1,0:T(8,128)(2,1)} %shard_map.29), calls=%async_computation | async-start | bytes 1572864 | tf_op jit(solution)/shard_map/all_to_all | solution.py:245
  18.1 0.0 collective-permute-done.2
  18.1 0.0 collective-permute-done.1
  18.2 1.3 %collective-permute-start.3 = (bf16[4,200,128]{2,1,0:T(8,128)(2,1)S(1)}, bf16[4,200,128]{2,1,0:T(8,128)(2,1)S(1)}, u32[]{:S(2)}, u32[]{:S(2)}) collective-permute-start(bf16[4,200,128]{2,1,0:T(8,128)(2,1)S(1)} %pad_maximum_fusion.1), channel_id=1, source_target_pairs={{0,6},{1,7},{2,0},{3,1},{4,2},{5,3},{6,4},{7,5},{16,18},{17,19},{1... | collective-permute-start | bytes 614408 | tf_op jit(solution)/shard_map/ppermute | solution.py:48
  19.4 7.7 %collective-permute-done.3 = bf16[4,200,128]{2,1,0:T(8,128)(2,1)S(1)} collective-permute-done((bf16[4,200,128]{2,1,0:T(8,128)(2,1)S(1)}, bf16[4,200,128]{2,1,0:T(8,128)(2,1)S(1)}, u32[]{:S(2)}, u32[]{:S(2)}) %collective-permute-start.3) | collective-permute-done | bytes 204832 | tf_op jit(solution)/shard_map/ppermute | solution.py:48
  27.2 0.4 collective-permute-start.4
  27.6 0.1 pad_add_fusion.rank_ref
  27.7 0.8 %shard_map.30 = (bf16[16,96,256]{2,1,0:T(8,128)(2,1)S(1)}, f32[16,96,128]{2,1,0:T(8,128)S(1)}, f32[1,128]{1,0:T(1,128)S(1)}) custom-call(s32[2]{0:T(128)S(1)} %pad_add_fusion.rank_ref, bf16[2,200,128]{2,1,0:T(8,128)(2,1)S(1)} %pad_maximum_fusion.2.pair_ref, bf16[7,200,128]{2,1,0:T(8,128)(2,1)S(1)} %pad_maximum_fusion.blocks_ref), custom_call_target="tpu_custom_call" | custom-call | tf_op jit(solution)/shard_map/pallas_call | solution.py:250
  28.5 0.5 collective-permute-done.4.blocks_ref
  28.9 0.7 %shard_map.31 = (bf16[16,96,256]{2,1,0:T(8,128)(2,1)S(1)}, f32[16,96,128]{2,1,0:T(8,128)S(1)}) custom-call(s32[2]{0:T(128)S(1)} %pad_add_fusion.rank_ref, bf16[7,200,128]{2,1,0:T(8,128)(2,1)S(1)} %collective-permute-done.4.blocks_ref, bf16[16,96,256]{2,1,0:T(8,128)(2,1)S(1)} %get-tuple-element.23.half_right_ref, ...), custom_call_target="tpu_custom_call", output_to_operand_aliasing={{0}: (2, {}), {1}: (3, {})} | custom-call | tf_op jit(solution)/shard_map/pallas_call | solution.py:257
  29.7 3.3 %all-to-all-done.left_ref = bf16[16,96,256]{2,1,0:T(8,128)(2,1)S(1)} async-done(((bf16[16,96,256]{2,1,0:T(8,128)(2,1)}), bf16[16,96,256]{2,1,0:T(8,128)(2,1)S(1)}, u32[]{:S(2)}, u32[]{:S(2)}) %all-to-all-start) | async-done | bytes 786464 | tf_op jit(solution)/shard_map/all_to_all | solution.py:245
  33.0 2.0 %shard_map.32 = (f32[1536,1536]{1,0:T(8,128)S(1)}, f32[16,1,1664]{2,1,0:T(1,128)S(1)}) custom-call(bf16[16,96,256]{2,1,0:T(8,128)(2,1)S(1)} %get-tuple-element.25.right_ref, f32[16,96,128]{2,1,0:T(8,128)S(1)} %get-tuple-element.26.columns_ref, f32[1,128]{1,0:T(1,128)S(1)} %get-tuple-element.27.mass_ref, bf16[16,96,256]{2,1,0:T(8,128)(2,1)S(1)} %all-to-all-done.left_ref), custom_call_target="tpu_custom_call" | custom-call | tf_op jit(solution)/shard_map/pallas_call | solution.py:266
  35.0 10.6 %all_to_all.20.got_ref = f32[16,1,1664]{2,1,0:T(1,128)S(1)} all-to-all(f32[16,1,1664]{2,1,0:T(1,128)S(1)} %get-tuple-element.30), channel_id=1, replica_groups=mesh['x'=4,'yl'=2,'k'=2,'yh'=2,'z'=8] {'x','yl','yh'}, dimensions={0} | all-to-all | bytes 212992 | tf_op jit(solution)/shard_map/all_to_all | solution.py:273
  45.6 1.6 %shard_map.33 = f32[16,1,1664]{2,1,0:T(1,128)S(1)} custom-call(s32[2]{0:T(128)S(1)} %pad_add_fusion.rank_ref, f32[1536,1536]{1,0:T(8,128)S(1)} %get-tuple-element.29.kernel_ref, f32[16,1,1664]{2,1,0:T(1,128)S(1)} %all_to_all.20.got_ref), custom_call_target="tpu_custom_call" | custom-call | tf_op jit(solution)/shard_map/pallas_call | solution.py:274
  47.2 13.6 %all_to_all.21.got_ref = f32[16,1,1664]{2,1,0:T(1,128)S(1)} all-to-all(f32[16,1,1664]{2,1,0:T(1,128)S(1)} %shard_map.33), channel_id=1, replica_groups=mesh['x'=4,'yl'=2,'k'=2,'yh'=2,'z'=8] {'k','z'}, dimensions={0} | all-to-all | bytes 212992 | tf_op jit(solution)/shard_map/all_to_all | solution.py:282
  60.8 1.7 %shard_map.34 = (f32[16,1,96]{2,1,0:T(1,128)S(1)}, f32[1,96]{1,0:T(1,128)S(1)}) custom-call(s32[2]{0:T(128)S(1)} %pad_add_fusion.rank_ref, f32[1536,1536]{1,0:T(8,128)S(1)} %get-tuple-element.29.kernel_ref, f32[16,1,1664]{2,1,0:T(1,128)S(1)} %all_to_all.21.got_ref), custom_call_target="tpu_custom_call" | custom-call | tf_op jit(solution)/shard_map/pallas_call | solution.py:283
  62.5 9.2 %all_to_all.22 = f32[16,1,96]{2,1,0:T(1,128)S(1)} all-to-all(f32[16,1,96]{2,1,0:T(1,128)S(1)} %get-tuple-element.32), channel_id=1, replica_groups=mesh['x'=4,'yl'=2,'k'=2,'yh'=2,'z'=8] {'x','yl','yh'}, dimensions={0} | all-to-all | bytes 12288 | tf_op jit(solution)/shard_map/all_to_all | solution.py:291
  71.8 0.5 fusion.1
  (4 shorter events, 0.1 us)
Async XLA Ops:
  0.9 4.4 %collective-permute-start = (bf16[200,128]{1,0:T(8,128)(2,1)S(1)}, bf16[200,128]{1,0:T(8,128)(2,1)S(1)}, u32[]{:S(2)}, u32[]{:S(2)}) collective-permute-start(bf16[200,128]{1,0:T(8,128)(2,1)S(1)} %shard_map.28.block_ref), channel_id=1, source_target_pairs={{0,16},{16,0},{1,17},{17,1},{2,18},{18,2},{3,19},{19,3},{4,20},{20... | collective-permute-start | bytes 153608 | tf_op jit(solution)/shard_map/ppermute | solution.py:238
  5.4 12.8 %collective-permute-start.1 = (bf16[2,200,128]{2,1,0:T(8,128)(2,1)S(1)}, bf16[2,200,128]{2,1,0:T(8,128)(2,1)S(1)}, u32[]{:S(2)}, u32[]{:S(2)}) collective-permute-start(bf16[2,200,128]{2,1,0:T(8,128)(2,1)S(1)} %pad_maximum_fusion.2.pair_ref), channel_id=1, source_target_pairs={{0,7},{1,0},{2,1},{3,2},{4,3},{5,4},{6,5},{7,6},{16,17},{17,18},{1... | collective-permute-start | bytes 307208 | tf_op jit(solution)/shard_map/ppermute | solution.py:48
  5.4 12.7 %collective-permute-start.2 = (bf16[200,128]{1,0:T(8,128)(2,1)S(1)}, bf16[200,128]{1,0:T(8,128)(2,1)S(1)}, u32[]{:S(2)}, u32[]{:S(2)}) collective-permute-start(bf16[200,128]{1,0:T(8,128)(2,1)S(1)} %shard_map.28.block_ref), channel_id=1, source_target_pairs={{0,4},{1,5},{2,6},{3,7},{4,0},{5,1},{6,2},{7,3},{8,12},{9,13},{10,... | collective-permute-start | bytes 153608 | tf_op jit(solution)/shard_map/ppermute | solution.py:241
  11.3 21.7 %all-to-all-start = ((bf16[16,96,256]{2,1,0:T(8,128)(2,1)}), bf16[16,96,256]{2,1,0:T(8,128)(2,1)S(1)}, u32[]{:S(2)}, u32[]{:S(2)}) async-start(bf16[16,96,256]{2,1,0:T(8,128)(2,1)} %shard_map.29), calls=%async_computation | async-start | bytes 1572864 | tf_op jit(solution)/shard_map/all_to_all | solution.py:245
  18.2 9.0 %collective-permute-start.3 = (bf16[4,200,128]{2,1,0:T(8,128)(2,1)S(1)}, bf16[4,200,128]{2,1,0:T(8,128)(2,1)S(1)}, u32[]{:S(2)}, u32[]{:S(2)}) collective-permute-start(bf16[4,200,128]{2,1,0:T(8,128)(2,1)S(1)} %pad_maximum_fusion.1), channel_id=1, source_target_pairs={{0,6},{1,7},{2,0},{3,1},{4,2},{5,3},{6,4},{7,5},{16,18},{17,19},{1... | collective-permute-start | bytes 614408 | tf_op jit(solution)/shard_map/ppermute | solution.py:48
  27.2 1.8 %collective-permute-start.4 = (bf16[7,200,128]{2,1,0:T(8,128)(2,1)S(1)}, bf16[7,200,128]{2,1,0:T(8,128)(2,1)S(1)}, u32[]{:S(2)}, u32[]{:S(2)}) collective-permute-start(bf16[7,200,128]{2,1,0:T(8,128)(2,1)S(1)} %pad_maximum_fusion.blocks_ref), channel_id=1, source_target_pairs={{0,16},{16,0},{1,17},{17,1},{2,18},{18,2},{3,19},{19,3},{4,20},{20... | collective-permute-start | bytes 1075208 | tf_op jit(solution)/shard_map/ppermute | solution.py:244

commit v6 on v5

--- a/solution.py
+++ b/solution.py
@@ -13,7 +13,7 @@
 AXES = ("x", "yl", "k", "yh", "z")
 ROW = ("x", "yl", "yh")
 COL = ("k", "z")
-SIDE = ((1, 0), (1, 1), (2, 0), (2, 1), (3, 0), (3, 1), (4, 0))
+SIDE = ((2, 0), (2, 1), (1, 0), (1, 1), (3, 0), (3, 1), (4, 0))
 LANES = 128
 TILE = 512
 ROWS = 768
@@ -237,10 +237,9 @@
     swap = [(0, 1), (1, 0)]
     other, send = lax.optimization_barrier((lax.ppermute(block, "k", swap), send))
     pair = jnp.stack([block, other])
-    first = along_z(pair, 1)
+    first = along_z(pair, 2)
     across = lax.ppermute(block, "z", [(z, z ^ 4) for z in range(8)])
-    pair, first, across = lax.optimization_barrier((pair, first, across))
-    side = jnp.concatenate([first, along_z(jnp.concatenate([pair, first]), 2), across[None]])
+    side = jnp.concatenate([first, along_z(jnp.concatenate([pair, first]), 1), across[None]])
     far = lax.ppermute(side, "k", swap)
     left = lax.all_to_all(send, ROW, 0, 0)
     ordered = [

time: 73.1 us -> 71.3 us (0.975)
  waiting for transfers between devices: 11.5 us -> 4.16 us
  starting transfers between devices: 17.7 us -> 20.9 us
  blocking collectives: 33.4 us -> 35.8 us
    ppermute x2, waiting for transfers between devices: 7.72 us -> 0.01 us  [along_z(): return lax.ppermute(array, ('k', 'z'), pairs)]
    ppermute x1, waiting for transfers between devices: 0.01 us -> 3.73 us  [shards(): across = lax.ppermute(block, 'z', [(z, z ^ 4) for z in range(8)])]
    all_to_all x1, waiting for transfers between devices: 3.33 us -> 0.01 us  [shards(): left = lax.all_to_all(send, ROW, 0, 0)]
    ppermute x1, starting transfers between devices: 0.41 us -> 3.58 us  [shards(): far = lax.ppermute(side, 'k', swap)]
    all_to_all x1, blocking collectives: 10.6 us -> 13.4 us  [shards(): got = lax.all_to_all(send, ROW, 0, 0)]
    ppermute x2, starting transfers between devices: 1.35 us -> 3.05 us  [along_z(): return lax.ppermute(array, ('k', 'z'), pairs)]
    ppermute x1, starting transfers between devices: 5.9 us -> 4.21 us  [shards(): across = lax.ppermute(block, 'z', [(z, z ^ 4) for z in range(8)])]
  transfers between devices with their start and end apart: 6 -> 6, of which waited for: 3 -> 2; matrix products, arithmetic and copies ran while one was open for 0% -> 0% of each run, Pallas kernels for 4% -> 4%
where the time goes in v6:
time: 71.3 us; the launch traced here: 70.5 us
  blocking collectives  35.8 us (50%)
  starting transfers between devices  20.9 us (29%)
  Pallas kernels  8.82 us (12%)
  waiting for transfers between devices  4.16 us (6%)
    all_to_all x1, blocking collectives, shards(): got = lax.all_to_all(send, ROW, 0, 0)  13.4 us
    all_to_all x1, blocking collectives, shards(): got = lax.all_to_all(send, COL, 0, 0)  13.2 us
    all_to_all x1, blocking collectives, shards(): sums = jnp.sum(lax.all_to_all(send, ROW, 0, 0), axis=0)  9.19 us
    all_to_all x1, starting transfers between devices, shards(): left = lax.all_to_all(send, ROW, 0, 0)  6.75 us
    ppermute x1, starting transfers between devices, shards(): across = lax.ppermute(block, 'z', [(z, z ^ 4) for z in range(8)])  4.21 us
    ppermute x1, waiting for transfers between devices, shards(): across = lax.ppermute(block, 'z', [(z, z ^ 4) for z in range(8)])  3.73 us
    ppermute x1, starting transfers between devices, shards(): far = lax.ppermute(side, 'k', swap)  3.58 us
    ppermute x1, starting transfers between devices, shards(): lax.ppermute(block, 'k', swap)  3.33 us
  transfers between devices with their start and end apart: 6, of which 2 were waited for; matrix products, arithmetic and copies ran while one was open for 0% of the time, Pallas kernels for 4%

profile of v6, /device:TPU:1, one launch (start us, length us, event | category | flops | bytes accessed | tf_op | source)
XLA Modules:
  0.0 70.5 jit_solution(7986043290400492592)
XLA Ops:
  0.0 0.9 %shard_map.28.block_ref = bf16[200,128]{1,0:T(8,128)(2,1)S(1)} custom-call(bf16[96,256]{1,0:T(8,128)(2,1)} %points_ref.1, f32[1,96]{1,0:T(1,128)} %bitcast.19), custom_call_target="tpu_custom_call" | custom-call | tf_op jit(solution)/shard_map/pallas_call | solution.py:217
  0.9 3.3 %collective-permute-start = (bf16[200,128]{1,0:T(8,128)(2,1)S(1)}, bf16[200,128]{1,0:T(8,128)(2,1)S(1)}, u32[]{:S(2)}, u32[]{:S(2)}) collective-permute-start(bf16[200,128]{1,0:T(8,128)(2,1)S(1)} %shard_map.28.block_ref), channel_id=1, source_target_pairs={{0,16},{16,0},{1,17},{17,1},{2,18},{18,2},{3,19},{19,3},{4,20},{20... | collective-permute-start | bytes 153608 | tf_op jit(solution)/shard_map/ppermute | solution.py:238
  4.3 1.0 %shard_map.29 = bf16[16,96,256]{2,1,0:T(8,128)(2,1)} custom-call(bf16[200,128]{1,0:T(8,128)(2,1)S(1)} %shard_map.28.block_ref), custom_call_target="tpu_custom_call" | custom-call | tf_op jit(solution)/shard_map/pallas_call | solution.py:229
  5.3 0.0 collective-permute-done
  5.4 1.3 %collective-permute-start.1 = (bf16[2,200,128]{2,1,0:T(8,128)(2,1)S(1)}, bf16[2,200,128]{2,1,0:T(8,128)(2,1)S(1)}, u32[]{:S(2)}, u32[]{:S(2)}) collective-permute-start(bf16[2,200,128]{2,1,0:T(8,128)(2,1)S(1)} %pad_maximum_fusion.2.pair_ref), channel_id=1, source_target_pairs={{0,6},{1,7},{2,0},{3,1},{4,2},{5,3},{6,4},{7,5},{16,18},{17,19},{1... | collective-permute-start | bytes 307208 | tf_op jit(solution)/shard_map/ppermute | solution.py:48
  6.7 6.8 %all-to-all-start = ((bf16[16,96,256]{2,1,0:T(8,128)(2,1)}), bf16[16,96,256]{2,1,0:T(8,128)(2,1)S(1)}, u32[]{:S(2)}, u32[]{:S(2)}) async-start(bf16[16,96,256]{2,1,0:T(8,128)(2,1)} %shard_map.29), calls=%async_computation | async-start | bytes 1572864 | tf_op jit(solution)/shard_map/all_to_all | solution.py:244
  13.4 0.0 collective-permute-done.1
  13.5 1.7 %collective-permute-start.2 = (bf16[4,200,128]{2,1,0:T(8,128)(2,1)S(1)}, bf16[4,200,128]{2,1,0:T(8,128)(2,1)S(1)}, u32[]{:S(2)}, u32[]{:S(2)}) collective-permute-start(bf16[4,200,128]{2,1,0:T(8,128)(2,1)S(1)} %pad_maximum_fusion.1), channel_id=1, source_target_pairs={{0,7},{1,0},{2,1},{3,2},{4,3},{5,4},{6,5},{7,6},{16,17},{17,18},{1... | collective-permute-start | bytes 614408 | tf_op jit(solution)/shard_map/ppermute | solution.py:48
  15.2 4.2 %collective-permute-start.3 = (bf16[200,128]{1,0:T(8,128)(2,1)S(1)}, bf16[200,128]{1,0:T(8,128)(2,1)S(1)}, u32[]{:S(2)}, u32[]{:S(2)}) collective-permute-start(bf16[200,128]{1,0:T(8,128)(2,1)S(1)} %shard_map.28.block_ref), channel_id=1, source_target_pairs={{0,4},{1,5},{2,6},{3,7},{4,0},{5,1},{6,2},{7,3},{8,12},{9,13},{10,... | collective-permute-start | bytes 153608 | tf_op jit(solution)/shard_map/ppermute | solution.py:241
  19.4 3.7 %collective-permute-done.3 = bf16[200,128]{1,0:T(8,128)(2,1)S(1)} collective-permute-done((bf16[200,128]{1,0:T(8,128)(2,1)S(1)}, bf16[200,128]{1,0:T(8,128)(2,1)S(1)}, u32[]{:S(2)}, u32[]{:S(2)}) %collective-permute-start.3) | collective-permute-done | bytes 51232 | tf_op jit(solution)/shard_map/ppermute | solution.py:241
  23.1 0.0 collective-permute-done.2
  23.2 3.6 %collective-permute-start.4 = (bf16[7,200,128]{2,1,0:T(8,128)(2,1)S(1)}, bf16[7,200,128]{2,1,0:T(8,128)(2,1)S(1)}, u32[]{:S(2)}, u32[]{:S(2)}) collective-permute-start(bf16[7,200,128]{2,1,0:T(8,128)(2,1)S(1)} %pad_maximum_fusion.blocks_ref), channel_id=1, source_target_pairs={{0,16},{16,0},{1,17},{17,1},{2,18},{18,2},{3,19},{19,3},{4,20},{20... | collective-permute-start | bytes 1075208 | tf_op jit(solution)/shard_map/ppermute | solution.py:243
  26.8 0.1 pad_add_fusion.rank_ref
  26.8 0.8 %shard_map.30 = (bf16[16,96,256]{2,1,0:T(8,128)(2,1)S(1)}, f32[16,96,128]{2,1,0:T(8,128)S(1)}, f32[1,128]{1,0:T(1,128)S(1)}) custom-call(s32[2]{0:T(128)S(1)} %pad_add_fusion.rank_ref, bf16[2,200,128]{2,1,0:T(8,128)(2,1)S(1)} %pad_maximum_fusion.2.pair_ref, bf16[7,200,128]{2,1,0:T(8,128)(2,1)S(1)} %pad_maximum_fusion.blocks_ref), custom_call_target="tpu_custom_call" | custom-call | tf_op jit(solution)/shard_map/pallas_call | solution.py:249
  27.6 0.4 collective-permute-done.4.blocks_ref
  28.1 0.7 %shard_map.31 = (bf16[16,96,256]{2,1,0:T(8,128)(2,1)S(1)}, f32[16,96,128]{2,1,0:T(8,128)S(1)}) custom-call(s32[2]{0:T(128)S(1)} %pad_add_fusion.rank_ref, bf16[7,200,128]{2,1,0:T(8,128)(2,1)S(1)} %collective-permute-done.4.blocks_ref, bf16[16,96,256]{2,1,0:T(8,128)(2,1)S(1)} %get-tuple-element.17.half_right_ref, ...), custom_call_target="tpu_custom_call", output_to_operand_aliasing={{0}: (2, {}), {1}: (3, {})} | custom-call | tf_op jit(solution)/shard_map/pallas_call | solution.py:256
  28.8 0.0 all-to-all-done.left_ref
  28.8 2.0 %shard_map.32 = (f32[1536,1536]{1,0:T(8,128)S(1)}, f32[16,1,1664]{2,1,0:T(1,128)S(1)}) custom-call(bf16[16,96,256]{2,1,0:T(8,128)(2,1)S(1)} %get-tuple-element.19.right_ref, f32[16,96,128]{2,1,0:T(8,128)S(1)} %get-tuple-element.20.columns_ref, f32[1,128]{1,0:T(1,128)S(1)} %get-tuple-element.21.mass_ref, bf16[16,96,256]{2,1,0:T(8,128)(2,1)S(1)} %all-to-all-done.left_ref), custom_call_target="tpu_custom_call" | custom-call | tf_op jit(solution)/shard_map/pallas_call | solution.py:265
  30.8 13.4 %all_to_all.20.got_ref = f32[16,1,1664]{2,1,0:T(1,128)S(1)} all-to-all(f32[16,1,1664]{2,1,0:T(1,128)S(1)} %get-tuple-element.24), channel_id=1, replica_groups=mesh['x'=4,'yl'=2,'k'=2,'yh'=2,'z'=8] {'x','yl','yh'}, dimensions={0} | all-to-all | bytes 212992 | tf_op jit(solution)/shard_map/all_to_all | solution.py:272
  44.2 1.6 %shard_map.33 = f32[16,1,1664]{2,1,0:T(1,128)S(1)} custom-call(s32[2]{0:T(128)S(1)} %pad_add_fusion.rank_ref, f32[1536,1536]{1,0:T(8,128)S(1)} %get-tuple-element.23.kernel_ref, f32[16,1,1664]{2,1,0:T(1,128)S(1)} %all_to_all.20.got_ref), custom_call_target="tpu_custom_call" | custom-call | tf_op jit(solution)/shard_map/pallas_call | solution.py:273
  45.8 13.2 %all_to_all.21.got_ref = f32[16,1,1664]{2,1,0:T(1,128)S(1)} all-to-all(f32[16,1,1664]{2,1,0:T(1,128)S(1)} %shard_map.33), channel_id=1, replica_groups=mesh['x'=4,'yl'=2,'k'=2,'yh'=2,'z'=8] {'k','z'}, dimensions={0} | all-to-all | bytes 212992 | tf_op jit(solution)/shard_map/all_to_all | solution.py:281
  59.0 1.7 %shard_map.34 = (f32[16,1,96]{2,1,0:T(1,128)S(1)}, f32[1,96]{1,0:T(1,128)S(1)}) custom-call(s32[2]{0:T(128)S(1)} %pad_add_fusion.rank_ref, f32[1536,1536]{1,0:T(8,128)S(1)} %get-tuple-element.23.kernel_ref, f32[16,1,1664]{2,1,0:T(1,128)S(1)} %all_to_all.21.got_ref), custom_call_target="tpu_custom_call" | custom-call | tf_op jit(solution)/shard_map/pallas_call | solution.py:282
  60.7 9.2 %all_to_all.22 = f32[16,1,96]{2,1,0:T(1,128)S(1)} all-to-all(f32[16,1,96]{2,1,0:T(1,128)S(1)} %get-tuple-element.26), channel_id=1, replica_groups=mesh['x'=4,'yl'=2,'k'=2,'yh'=2,'z'=8] {'x','yl','yh'}, dimensions={0} | all-to-all | bytes 12288 | tf_op jit(solution)/shard_map/all_to_all | solution.py:290
  69.9 0.5 fusion.1
  (4 shorter events, 0.1 us)
Async XLA Ops:
  0.9 4.4 %collective-permute-start = (bf16[200,128]{1,0:T(8,128)(2,1)S(1)}, bf16[200,128]{1,0:T(8,128)(2,1)S(1)}, u32[]{:S(2)}, u32[]{:S(2)}) collective-permute-start(bf16[200,128]{1,0:T(8,128)(2,1)S(1)} %shard_map.28.block_ref), channel_id=1, source_target_pairs={{0,16},{16,0},{1,17},{17,1},{2,18},{18,2},{3,19},{19,3},{4,20},{20... | collective-permute-start | bytes 153608 | tf_op jit(solution)/shard_map/ppermute | solution.py:238
  5.4 8.1 %collective-permute-start.1 = (bf16[2,200,128]{2,1,0:T(8,128)(2,1)S(1)}, bf16[2,200,128]{2,1,0:T(8,128)(2,1)S(1)}, u32[]{:S(2)}, u32[]{:S(2)}) collective-permute-start(bf16[2,200,128]{2,1,0:T(8,128)(2,1)S(1)} %pad_maximum_fusion.2.pair_ref), channel_id=1, source_target_pairs={{0,6},{1,7},{2,0},{3,1},{4,2},{5,3},{6,4},{7,5},{16,18},{17,19},{1... | collective-permute-start | bytes 307208 | tf_op jit(solution)/shard_map/ppermute | solution.py:48
  6.7 22.1 %all-to-all-start = ((bf16[16,96,256]{2,1,0:T(8,128)(2,1)}), bf16[16,96,256]{2,1,0:T(8,128)(2,1)S(1)}, u32[]{:S(2)}, u32[]{:S(2)}) async-start(bf16[16,96,256]{2,1,0:T(8,128)(2,1)} %shard_map.29), calls=%async_computation | async-start | bytes 1572864 | tf_op jit(solution)/shard_map/all_to_all | solution.py:244
  13.5 9.7 %collective-permute-start.2 = (bf16[4,200,128]{2,1,0:T(8,128)(2,1)S(1)}, bf16[4,200,128]{2,1,0:T(8,128)(2,1)S(1)}, u32[]{:S(2)}, u32[]{:S(2)}) collective-permute-start(bf16[4,200,128]{2,1,0:T(8,128)(2,1)S(1)} %pad_maximum_fusion.1), channel_id=1, source_target_pairs={{0,7},{1,0},{2,1},{3,2},{4,3},{5,4},{6,5},{7,6},{16,17},{17,18},{1... | collective-permute-start | bytes 614408 | tf_op jit(solution)/shard_map/ppermute | solution.py:48
  15.2 7.9 %collective-permute-start.3 = (bf16[200,128]{1,0:T(8,128)(2,1)S(1)}, bf16[200,128]{1,0:T(8,128)(2,1)S(1)}, u32[]{:S(2)}, u32[]{:S(2)}) collective-permute-start(bf16[200,128]{1,0:T(8,128)(2,1)S(1)} %shard_map.28.block_ref), channel_id=1, source_target_pairs={{0,4},{1,5},{2,6},{3,7},{4,0},{5,1},{6,2},{7,3},{8,12},{9,13},{10,... | collective-permute-start | bytes 153608 | tf_op jit(solution)/shard_map/ppermute | solution.py:241
  23.2 4.9 %collective-permute-start.4 = (bf16[7,200,128]{2,1,0:T(8,128)(2,1)S(1)}, bf16[7,200,128]{2,1,0:T(8,128)(2,1)S(1)}, u32[]{:S(2)}, u32[]{:S(2)}) collective-permute-start(bf16[7,200,128]{2,1,0:T(8,128)(2,1)S(1)} %pad_maximum_fusion.blocks_ref), channel_id=1, source_target_pairs={{0,16},{16,0},{1,17},{17,1},{2,18},{18,2},{3,19},{19,3},{4,20},{20... | collective-permute-start | bytes 1075208 | tf_op jit(solution)/shard_map/ppermute | solution.py:243

commit v7 on v6

--- a/solution.py
+++ b/solution.py
@@ -13,7 +13,7 @@
 AXES = ("x", "yl", "k", "yh", "z")
 ROW = ("x", "yl", "yh")
 COL = ("k", "z")
-SIDE = ((2, 0), (2, 1), (1, 0), (1, 1), (3, 0), (3, 1), (4, 0))
+SIDE = ((2, 0), (2, 1), (1, 0), (1, 1), (3, 0), (3, 1))
 LANES = 128
 TILE = 512
 ROWS = 768
@@ -105,8 +105,9 @@
     mass_ref[...] = jnp.sum(extra[3:6], axis=0, keepdims=True)
 
 
-def far_kernel(rank_ref, blocks_ref, half_right_ref, half_columns_ref, right_ref, columns_ref):
+def far_kernel(rank_ref, blocks_ref, last_ref, half_right_ref, half_columns_ref, right_ref, columns_ref):
     core, z = rank_ref[1] // 8, rank_ref[1] % 8
+    place_blocks(last_ref, ((4, 0), (4, 1)), core, z, right_ref, columns_ref)
     place_blocks(blocks_ref, SIDE, 1 - core, z, right_ref, columns_ref)
 
 
@@ -169,12 +170,12 @@
     weight = jnp.concatenate([growth[n : n + 1] * mass[:, piece] for n, piece in enumerate(lane_pieces(length))], axis=1)
 
     def step(n, carry):
-        rows = pl.ds(pl.multiple_of(n * 256, 256), 256)
+        rows = pl.ds(pl.multiple_of(n * 512, 512), 512)
         weighted = kernel_ref[rows, :] * weight
         partial[rows, :] = sum(weighted[:, piece] for piece in lane_pieces(length))
         return carry
 
-    lax.fori_loop(0, length // 256, step, 0)
+    lax.fori_loop(0, length // 512, step, 0)
     own_mass = got_ref[rank_ref[0], :, length:] * (1.0 / total)
     mine = own_piece(flat, rank_ref[0], own) + jnp.log(own_mass)
     pieces = [row_of_sums(partial[piece, :]) for piece in lane_pieces(length)]
@@ -200,7 +201,7 @@
         weighted = kernel_ref[rows, :] * repeated(columns[rows, :], length)
         return sums + (weighted[:8] + weighted[8:])
 
-    sums = lax.fori_loop(0, length // 16, step, jnp.zeros((8, length), jnp.float32), unroll=4)
+    sums = lax.fori_loop(0, length // 16, step, jnp.zeros((8, length), jnp.float32), unroll=8)
     sums = jnp.sum(sums, axis=0, keepdims=True)
     for d in range(groups):
         send_ref[d] = sums[:, d * own : (d + 1) * own]
@@ -238,8 +239,9 @@
     other, send = lax.optimization_barrier((lax.ppermute(block, "k", swap), send))
     pair = jnp.stack([block, other])
     first = along_z(pair, 2)
-    across = lax.ppermute(block, "z", [(z, z ^ 4) for z in range(8)])
-    side = jnp.concatenate([first, along_z(jnp.concatenate([pair, first]), 1), across[None]])
+    last, second = along_z(first, 2), along_z(jnp.concatenate([pair, first]), 1)
+    last, second = lax.optimization_barrier((last, second))
+    side = jnp.concatenate([first, second])
     far = lax.ppermute(side, "k", swap)
     left = lax.all_to_all(send, ROW, 0, 0)
     ordered = [
@@ -256,11 +258,11 @@
     right, columns = pl.pallas_call(
         far_kernel,
         out_shape=ordered,
-        in_specs=[SMEM, VMEM, VMEM, VMEM],
+        in_specs=[SMEM] + [VMEM] * 4,
         out_specs=[VMEM, VMEM],
-        input_output_aliases={2: 0, 3: 1},
-        compiler_params=PARAMS,
-    )(ranks, far, right, columns)
+        input_output_aliases={3: 0, 4: 1},
+        compiler_params=PARAMS,
+    )(ranks, far, last, right, columns)
     message = jax.ShapeDtypeStruct((groups, 1, length + LANES), f32)
     kernel, send = pl.pallas_call(
         build_kernel,

time: 71.3 us -> 70.9 us (level)
  starting transfers between devices: 20.9 us -> 19.3 us
    ppermute x2 -> x3, waiting for transfers between devices: 0.01 us -> 4.48 us  [along_z(): return lax.ppermute(array, ('k', 'z'), pairs)]
    ppermute x1 -> x0, starting transfers between devices: 4.21 us -> none  [shards(): across = lax.ppermute(block, 'z', [(z, z ^ 4) for z in range(8)])]
    ppermute x1 -> x0, waiting for transfers between devices: 3.73 us -> none  [shards(): across = lax.ppermute(block, 'z', [(z, z ^ 4) for z in range(8)])]
    ppermute x2 -> x3, starting transfers between devices: 3.05 us -> 6.35 us  [along_z(): return lax.ppermute(array, ('k', 'z'), pairs)]
    ppermute x1, starting transfers between devices: 3.58 us -> 2.83 us  [shards(): far = lax.ppermute(side, 'k', swap)]
where the time goes in v7:
time: 70.9 us; the launch traced here: 70.1 us
  blocking collectives  36.4 us (51%)
  starting transfers between devices  19.3 us (27%)
  Pallas kernels  8.7 us (12%)
  waiting for transfers between devices  4.87 us (7%)
    all_to_all x1, blocking collectives, shards(): got = lax.all_to_all(send, ROW, 0, 0)  13.7 us
    all_to_all x1, blocking collectives, shards(): got = lax.all_to_all(send, COL, 0, 0)  13.6 us
    all_to_all x1, blocking collectives, shards(): sums = jnp.sum(lax.all_to_all(send, ROW, 0, 0), axis=0)  9.19 us
    all_to_all x1, starting transfers between devices, shards(): left = lax.all_to_all(send, ROW, 0, 0)  6.75 us
    ppermute x3, starting transfers between devices, along_z(): return lax.ppermute(array, ('k', 'z'), pairs)  6.35 us
    ppermute x3, waiting for transfers between devices, along_z(): return lax.ppermute(array, ('k', 'z'), pairs)  4.48 us
    ppermute x1, starting transfers between devices, shards(): lax.ppermute(block, 'k', swap)  3.33 us
    ppermute x1, starting transfers between devices, shards(): far = lax.ppermute(side, 'k', swap)  2.83 us
  transfers between devices with their start and end apart: 6, of which 2 were waited for; matrix products, arithmetic and copies ran while one was open for 0% of the time, Pallas kernels for 4%

profile of v7, /device:TPU:1, one launch (start us, length us, event | category | flops | bytes accessed | tf_op | source)
XLA Modules:
  0.0 70.1 jit_solution(3094615406361747813)
XLA Ops:
  0.0 0.9 %shard_map.28.block_ref = bf16[200,128]{1,0:T(8,128)(2,1)S(1)} custom-call(bf16[96,256]{1,0:T(8,128)(2,1)} %points_ref.1, f32[1,96]{1,0:T(1,128)} %bitcast.17), custom_call_target="tpu_custom_call" | custom-call | tf_op jit(solution)/shard_map/pallas_call | solution.py:218
  0.9 3.3 %collective-permute-start = (bf16[200,128]{1,0:T(8,128)(2,1)S(1)}, bf16[200,128]{1,0:T(8,128)(2,1)S(1)}, u32[]{:S(2)}, u32[]{:S(2)}) collective-permute-start(bf16[200,128]{1,0:T(8,128)(2,1)S(1)} %shard_map.28.block_ref), channel_id=1, source_target_pairs={{0,16},{16,0},{1,17},{17,1},{2,18},{18,2},{3,19},{19,3},{4,20},{20... | collective-permute-start | bytes 153608 | tf_op jit(solution)/shard_map/ppermute | solution.py:239
  4.3 1.0 %shard_map.29 = bf16[16,96,256]{2,1,0:T(8,128)(2,1)} custom-call(bf16[200,128]{1,0:T(8,128)(2,1)S(1)} %shard_map.28.block_ref), custom_call_target="tpu_custom_call" | custom-call | tf_op jit(solution)/shard_map/pallas_call | solution.py:230
  5.3 0.0 collective-permute-done
  5.4 1.3 %collective-permute-start.1 = (bf16[2,200,128]{2,1,0:T(8,128)(2,1)S(1)}, bf16[2,200,128]{2,1,0:T(8,128)(2,1)S(1)}, u32[]{:S(2)}, u32[]{:S(2)}) collective-permute-start(bf16[2,200,128]{2,1,0:T(8,128)(2,1)S(1)} %pad_maximum_fusion.1.pair_ref), channel_id=1, source_target_pairs={{0,6},{1,7},{2,0},{3,1},{4,2},{5,3},{6,4},{7,5},{16,18},{17,19},{1... | collective-permute-start | bytes 307208 | tf_op jit(solution)/shard_map/ppermute | solution.py:48
  6.7 6.8 %all-to-all-start = ((bf16[16,96,256]{2,1,0:T(8,128)(2,1)}), bf16[16,96,256]{2,1,0:T(8,128)(2,1)S(1)}, u32[]{:S(2)}, u32[]{:S(2)}) async-start(bf16[16,96,256]{2,1,0:T(8,128)(2,1)} %shard_map.29), calls=%async_computation | async-start | bytes 1572864 | tf_op jit(solution)/shard_map/all_to_all | solution.py:246
  13.4 0.0 collective-permute-done.1
  13.5 1.7 %collective-permute-start.3 = (bf16[4,200,128]{2,1,0:T(8,128)(2,1)S(1)}, bf16[4,200,128]{2,1,0:T(8,128)(2,1)S(1)}, u32[]{:S(2)}, u32[]{:S(2)}) collective-permute-start(bf16[4,200,128]{2,1,0:T(8,128)(2,1)S(1)} %pad_maximum_fusion), channel_id=1, source_target_pairs={{0,7},{1,0},{2,1},{3,2},{4,3},{5,4},{6,5},{7,6},{16,17},{17,18},{1... | collective-permute-start | bytes 614408 | tf_op jit(solution)/shard_map/ppermute | solution.py:48
  15.2 3.3 %collective-permute-start.2 = (bf16[2,200,128]{2,1,0:T(8,128)(2,1)S(1)}, bf16[2,200,128]{2,1,0:T(8,128)(2,1)S(1)}, u32[]{:S(2)}, u32[]{:S(2)}) collective-permute-start(bf16[2,200,128]{2,1,0:T(8,128)(2,1)S(1)} %collective-permute-done.1), channel_id=1, source_target_pairs={{0,6},{1,7},{2,0},{3,1},{4,2},{5,3},{6,4},{7,5},{16,18},{17,19},{1... | collective-permute-start | bytes 307208 | tf_op jit(solution)/shard_map/ppermute | solution.py:48
  18.5 4.5 %collective-permute-done.2.last_ref = bf16[2,200,128]{2,1,0:T(8,128)(2,1)S(1)} collective-permute-done((bf16[2,200,128]{2,1,0:T(8,128)(2,1)S(1)}, bf16[2,200,128]{2,1,0:T(8,128)(2,1)S(1)}, u32[]{:S(2)}, u32[]{:S(2)}) %collective-permute-start.2) | collective-permute-done | bytes 102432 | tf_op jit(solution)/shard_map/ppermute | solution.py:48
  23.0 0.0 collective-permute-done.3
  23.0 2.8 %collective-permute-start.4 = (bf16[6,200,128]{2,1,0:T(8,128)(2,1)S(1)}, bf16[6,200,128]{2,1,0:T(8,128)(2,1)S(1)}, u32[]{:S(2)}, u32[]{:S(2)}) collective-permute-start(bf16[6,200,128]{2,1,0:T(8,128)(2,1)S(1)} %constant_dynamic-update-slice_fusion.blocks_ref), channel_id=1, source_target_pairs={{0,16},{16,0},{1,17},{17,1},{2,18},{18,2},{3,19},{19,3},{4,20},{20... | collective-permute-start | bytes 921608 | tf_op jit(solution)/shard_map/ppermute | solution.py:245
  25.9 0.1 pad_add_fusion.rank_ref
  25.9 0.8 %shard_map.30 = (bf16[16,96,256]{2,1,0:T(8,128)(2,1)S(1)}, f32[16,96,128]{2,1,0:T(8,128)S(1)}, f32[1,128]{1,0:T(1,128)S(1)}) custom-call(s32[2]{0:T(128)S(1)} %pad_add_fusion.rank_ref, bf16[2,200,128]{2,1,0:T(8,128)(2,1)S(1)} %pad_maximum_fusion.1.pair_ref, bf16[6,200,128]{2,1,0:T(8,128)(2,1)S(1)} %constant_dynamic-update-slice_fusion.blocks_ref), custom_call_target="tpu_custom_call" | custom-call | tf_op jit(solution)/shard_map/pallas_call | solution.py:251
  26.7 0.4 collective-permute-done.4.blocks_ref
  27.1 0.8 %shard_map.31 = (bf16[16,96,256]{2,1,0:T(8,128)(2,1)S(1)}, f32[16,96,128]{2,1,0:T(8,128)S(1)}) custom-call(s32[2]{0:T(128)S(1)} %pad_add_fusion.rank_ref, bf16[6,200,128]{2,1,0:T(8,128)(2,1)S(1)} %collective-permute-done.4.blocks_ref, bf16[2,200,128]{2,1,0:T(8,128)(2,1)S(1)} %collective-permute-done.2.last_ref, ...), custom_call_target="tpu_custom_call", output_to_operand_aliasing={{0}: (3, {}), {1}: (4, {})} | custom-call | tf_op jit(solution)/shard_map/pallas_call | solution.py:258
  27.8 0.0 all-to-all-done.left_ref
  27.9 2.0 %shard_map.32 = (f32[1536,1536]{1,0:T(8,128)S(1)}, f32[16,1,1664]{2,1,0:T(1,128)S(1)}) custom-call(bf16[16,96,256]{2,1,0:T(8,128)(2,1)S(1)} %get-tuple-element.23.right_ref, f32[16,96,128]{2,1,0:T(8,128)S(1)} %get-tuple-element.24.columns_ref, f32[1,128]{1,0:T(1,128)S(1)} %get-tuple-element.25.mass_ref, bf16[16,96,256]{2,1,0:T(8,128)(2,1)S(1)} %all-to-all-done.left_ref), custom_call_target="tpu_custom_call" | custom-call | tf_op jit(solution)/shard_map/pallas_call | solution.py:267
  29.8 13.7 %all_to_all.20.got_ref = f32[16,1,1664]{2,1,0:T(1,128)S(1)} all-to-all(f32[16,1,1664]{2,1,0:T(1,128)S(1)} %get-tuple-element.28), channel_id=1, replica_groups=mesh['x'=4,'yl'=2,'k'=2,'yh'=2,'z'=8] {'x','yl','yh'}, dimensions={0} | all-to-all | bytes 212992 | tf_op jit(solution)/shard_map/all_to_all | solution.py:274
  43.5 1.6 %shard_map.33 = f32[16,1,1664]{2,1,0:T(1,128)S(1)} custom-call(s32[2]{0:T(128)S(1)} %pad_add_fusion.rank_ref, f32[1536,1536]{1,0:T(8,128)S(1)} %get-tuple-element.27.kernel_ref, f32[16,1,1664]{2,1,0:T(1,128)S(1)} %all_to_all.20.got_ref), custom_call_target="tpu_custom_call" | custom-call | tf_op jit(solution)/shard_map/pallas_call | solution.py:275
  45.1 13.6 %all_to_all.21.got_ref = f32[16,1,1664]{2,1,0:T(1,128)S(1)} all-to-all(f32[16,1,1664]{2,1,0:T(1,128)S(1)} %shard_map.33), channel_id=1, replica_groups=mesh['x'=4,'yl'=2,'k'=2,'yh'=2,'z'=8] {'k','z'}, dimensions={0} | all-to-all | bytes 212992 | tf_op jit(solution)/shard_map/all_to_all | solution.py:283
  58.7 1.7 %shard_map.34 = (f32[16,1,96]{2,1,0:T(1,128)S(1)}, f32[1,96]{1,0:T(1,128)S(1)}) custom-call(s32[2]{0:T(128)S(1)} %pad_add_fusion.rank_ref, f32[1536,1536]{1,0:T(8,128)S(1)} %get-tuple-element.27.kernel_ref, f32[16,1,1664]{2,1,0:T(1,128)S(1)} %all_to_all.21.got_ref), custom_call_target="tpu_custom_call" | custom-call | tf_op jit(solution)/shard_map/pallas_call | solution.py:284
  60.3 9.2 %all_to_all.22 = f32[16,1,96]{2,1,0:T(1,128)S(1)} all-to-all(f32[16,1,96]{2,1,0:T(1,128)S(1)} %get-tuple-element.30), channel_id=1, replica_groups=mesh['x'=4,'yl'=2,'k'=2,'yh'=2,'z'=8] {'x','yl','yh'}, dimensions={0} | all-to-all | bytes 12288 | tf_op jit(solution)/shard_map/all_to_all | solution.py:292
  69.6 0.5 fusion.1
  (5 shorter events, 0.1 us)
Async XLA Ops:
  0.9 4.4 %collective-permute-start = (bf16[200,128]{1,0:T(8,128)(2,1)S(1)}, bf16[200,128]{1,0:T(8,128)(2,1)S(1)}, u32[]{:S(2)}, u32[]{:S(2)}) collective-permute-start(bf16[200,128]{1,0:T(8,128)(2,1)S(1)} %shard_map.28.block_ref), channel_id=1, source_target_pairs={{0,16},{16,0},{1,17},{17,1},{2,18},{18,2},{3,19},{19,3},{4,20},{20... | collective-permute-start | bytes 153608 | tf_op jit(solution)/shard_map/ppermute | solution.py:239
  5.4 8.1 %collective-permute-start.1 = (bf16[2,200,128]{2,1,0:T(8,128)(2,1)S(1)}, bf16[2,200,128]{2,1,0:T(8,128)(2,1)S(1)}, u32[]{:S(2)}, u32[]{:S(2)}) collective-permute-start(bf16[2,200,128]{2,1,0:T(8,128)(2,1)S(1)} %pad_maximum_fusion.1.pair_ref), channel_id=1, source_target_pairs={{0,6},{1,7},{2,0},{3,1},{4,2},{5,3},{6,4},{7,5},{16,18},{17,19},{1... | collective-permute-start | bytes 307208 | tf_op jit(solution)/shard_map/ppermute | solution.py:48
  6.7 21.2 %all-to-all-start = ((bf16[16,96,256]{2,1,0:T(8,128)(2,1)}), bf16[16,96,256]{2,1,0:T(8,128)(2,1)S(1)}, u32[]{:S(2)}, u32[]{:S(2)}) async-start(bf16[16,96,256]{2,1,0:T(8,128)(2,1)} %shard_map.29), calls=%async_computation | async-start | bytes 1572864 | tf_op jit(solution)/shard_map/all_to_all | solution.py:246
  13.5 9.5 %collective-permute-start.3 = (bf16[4,200,128]{2,1,0:T(8,128)(2,1)S(1)}, bf16[4,200,128]{2,1,0:T(8,128)(2,1)S(1)}, u32[]{:S(2)}, u32[]{:S(2)}) collective-permute-start(bf16[4,200,128]{2,1,0:T(8,128)(2,1)S(1)} %pad_maximum_fusion), channel_id=1, source_target_pairs={{0,7},{1,0},{2,1},{3,2},{4,3},{5,4},{6,5},{7,6},{16,17},{17,18},{1... | collective-permute-start | bytes 614408 | tf_op jit(solution)/shard_map/ppermute | solution.py:48
  15.2 7.8 %collective-permute-start.2 = (bf16[2,200,128]{2,1,0:T(8,128)(2,1)S(1)}, bf16[2,200,128]{2,1,0:T(8,128)(2,1)S(1)}, u32[]{:S(2)}, u32[]{:S(2)}) collective-permute-start(bf16[2,200,128]{2,1,0:T(8,128)(2,1)S(1)} %collective-permute-done.1), channel_id=1, source_target_pairs={{0,6},{1,7},{2,0},{3,1},{4,2},{5,3},{6,4},{7,5},{16,18},{17,19},{1... | collective-permute-start | bytes 307208 | tf_op jit(solution)/shard_map/ppermute | solution.py:48
  23.0 4.1 %collective-permute-start.4 = (bf16[6,200,128]{2,1,0:T(8,128)(2,1)S(1)}, bf16[6,200,128]{2,1,0:T(8,128)(2,1)S(1)}, u32[]{:S(2)}, u32[]{:S(2)}) collective-permute-start(bf16[6,200,128]{2,1,0:T(8,128)(2,1)S(1)} %constant_dynamic-update-slice_fusion.blocks_ref), channel_id=1, source_target_pairs={{0,16},{16,0},{1,17},{17,1},{2,18},{18,2},{3,19},{19,3},{4,20},{20... | collective-permute-start | bytes 921608 | tf_op jit(solution)/shard_map/ppermute | solution.py:245

commit v8 on v7

--- a/solution.py
+++ b/solution.py
@@ -204,7 +204,7 @@
     sums = lax.fori_loop(0, length // 16, step, jnp.zeros((8, length), jnp.float32), unroll=8)
     sums = jnp.sum(sums, axis=0, keepdims=True)
     for d in range(groups):
-        send_ref[d] = sums[:, d * own : (d + 1) * own]
+        send_ref[d] = jnp.concatenate([sums[:, d * own : (d + 1) * own], jnp.zeros((1, LANES - own), jnp.float32)], axis=1)
     mine_ref[...] = own_piece(flat, rank_ref[1], own)[:, :own]
 
 
@@ -283,13 +283,13 @@
     got = lax.all_to_all(send, COL, 0, 0)
     send, mine = pl.pallas_call(
         functools.partial(column_sums_kernel, own),
-        out_shape=[jax.ShapeDtypeStruct((groups, 1, own), f32), jax.ShapeDtypeStruct((1, own), f32)],
+        out_shape=[jax.ShapeDtypeStruct((groups, 1, LANES), f32), jax.ShapeDtypeStruct((1, own), f32)],
         in_specs=[SMEM, VMEM, VMEM],
         out_specs=[VMEM, VMEM],
         scratch_shapes=[pltpu.VMEM((length, LANES), f32), pltpu.VMEM((16, LANES), f32)],
         compiler_params=PARAMS,
     )(ranks, kernel, got)
-    sums = jnp.sum(lax.all_to_all(send, ROW, 0, 0), axis=0)
+    sums = jnp.sum(lax.all_to_all(send, ROW, 0, 0), axis=0)[:, :own]
     return (0.5 * (mine - jnp.log(sums))).reshape(own)
 
 

time: 70.9 us -> 70.9 us (level)
  no operation moved by 1% of the time
where the time goes in v8:
time: 70.9 us; the launch traced here: 70.1 us
  blocking collectives  36.4 us (51%)
  starting transfers between devices  19.3 us (27%)
  Pallas kernels  8.7 us (12%)
  waiting for transfers between devices  4.87 us (7%)
    all_to_all x1, blocking collectives, shards(): got = lax.all_to_all(send, ROW, 0, 0)  13.7 us
    all_to_all x1, blocking collectives, shards(): got = lax.all_to_all(send, COL, 0, 0)  13.6 us
    all_to_all x1, blocking collectives, shards(): sums = jnp.sum(lax.all_to_all(send, ROW, 0, 0), axis=0)[:, :own]  9.19 us
    all_to_all x1, starting transfers between devices, shards(): left = lax.all_to_all(send, ROW, 0, 0)  6.75 us
    ppermute x3, starting transfers between devices, along_z(): return lax.ppermute(array, ('k', 'z'), pairs)  6.35 us
    ppermute x3, waiting for transfers between devices, along_z(): return lax.ppermute(array, ('k', 'z'), pairs)  4.48 us
    ppermute x1, starting transfers between devices, shards(): lax.ppermute(block, 'k', swap)  3.33 us
    ppermute x1, starting transfers between devices, shards(): far = lax.ppermute(side, 'k', swap)  2.83 us
  transfers between devices with their start and end apart: 6, of which 2 were waited for; matrix products, arithmetic and copies ran while one was open for 0% of the time, Pallas kernels for 4%

profile of v8, /device:TPU:1, one launch (start us, length us, event | category | flops | bytes accessed | tf_op | source)
XLA Modules:
  0.0 70.1 jit_solution(6463297092118948551)
XLA Ops:
  0.0 0.9 %shard_map.28.block_ref = bf16[200,128]{1,0:T(8,128)(2,1)S(1)} custom-call(bf16[96,256]{1,0:T(8,128)(2,1)} %points_ref.1, f32[1,96]{1,0:T(1,128)} %bitcast.12), custom_call_target="tpu_custom_call" | custom-call | tf_op jit(solution)/shard_map/pallas_call | solution.py:218
  0.9 3.3 %collective-permute-start = (bf16[200,128]{1,0:T(8,128)(2,1)S(1)}, bf16[200,128]{1,0:T(8,128)(2,1)S(1)}, u32[]{:S(2)}, u32[]{:S(2)}) collective-permute-start(bf16[200,128]{1,0:T(8,128)(2,1)S(1)} %shard_map.28.block_ref), channel_id=1, source_target_pairs={{0,16},{16,0},{1,17},{17,1},{2,18},{18,2},{3,19},{19,3},{4,20},{20... | collective-permute-start | bytes 153608 | tf_op jit(solution)/shard_map/ppermute | solution.py:239
  4.3 1.0 %shard_map.29 = bf16[16,96,256]{2,1,0:T(8,128)(2,1)} custom-call(bf16[200,128]{1,0:T(8,128)(2,1)S(1)} %shard_map.28.block_ref), custom_call_target="tpu_custom_call" | custom-call | tf_op jit(solution)/shard_map/pallas_call | solution.py:230
  5.3 0.0 collective-permute-done
  5.4 1.3 %collective-permute-start.1 = (bf16[2,200,128]{2,1,0:T(8,128)(2,1)S(1)}, bf16[2,200,128]{2,1,0:T(8,128)(2,1)S(1)}, u32[]{:S(2)}, u32[]{:S(2)}) collective-permute-start(bf16[2,200,128]{2,1,0:T(8,128)(2,1)S(1)} %pad_maximum_fusion.1.pair_ref), channel_id=1, source_target_pairs={{0,6},{1,7},{2,0},{3,1},{4,2},{5,3},{6,4},{7,5},{16,18},{17,19},{1... | collective-permute-start | bytes 307208 | tf_op jit(solution)/shard_map/ppermute | solution.py:48
  6.7 6.8 %all-to-all-start = ((bf16[16,96,256]{2,1,0:T(8,128)(2,1)}), bf16[16,96,256]{2,1,0:T(8,128)(2,1)S(1)}, u32[]{:S(2)}, u32[]{:S(2)}) async-start(bf16[16,96,256]{2,1,0:T(8,128)(2,1)} %shard_map.29), calls=%async_computation | async-start | bytes 1572864 | tf_op jit(solution)/shard_map/all_to_all | solution.py:246
  13.4 0.0 collective-permute-done.1
  13.5 1.7 %collective-permute-start.3 = (bf16[4,200,128]{2,1,0:T(8,128)(2,1)S(1)}, bf16[4,200,128]{2,1,0:T(8,128)(2,1)S(1)}, u32[]{:S(2)}, u32[]{:S(2)}) collective-permute-start(bf16[4,200,128]{2,1,0:T(8,128)(2,1)S(1)} %pad_maximum_fusion), channel_id=1, source_target_pairs={{0,7},{1,0},{2,1},{3,2},{4,3},{5,4},{6,5},{7,6},{16,17},{17,18},{1... | collective-permute-start | bytes 614408 | tf_op jit(solution)/shard_map/ppermute | solution.py:48
  15.2 3.3 %collective-permute-start.2 = (bf16[2,200,128]{2,1,0:T(8,128)(2,1)S(1)}, bf16[2,200,128]{2,1,0:T(8,128)(2,1)S(1)}, u32[]{:S(2)}, u32[]{:S(2)}) collective-permute-start(bf16[2,200,128]{2,1,0:T(8,128)(2,1)S(1)} %collective-permute-done.1), channel_id=1, source_target_pairs={{0,6},{1,7},{2,0},{3,1},{4,2},{5,3},{6,4},{7,5},{16,18},{17,19},{1... | collective-permute-start | bytes 307208 | tf_op jit(solution)/shard_map/ppermute | solution.py:48
  18.5 4.5 %collective-permute-done.2.last_ref = bf16[2,200,128]{2,1,0:T(8,128)(2,1)S(1)} collective-permute-done((bf16[2,200,128]{2,1,0:T(8,128)(2,1)S(1)}, bf16[2,200,128]{2,1,0:T(8,128)(2,1)S(1)}, u32[]{:S(2)}, u32[]{:S(2)}) %collective-permute-start.2) | collective-permute-done | bytes 102432 | tf_op jit(solution)/shard_map/ppermute | solution.py:48
  23.0 0.0 collective-permute-done.3
  23.0 2.8 %collective-permute-start.4 = (bf16[6,200,128]{2,1,0:T(8,128)(2,1)S(1)}, bf16[6,200,128]{2,1,0:T(8,128)(2,1)S(1)}, u32[]{:S(2)}, u32[]{:S(2)}) collective-permute-start(bf16[6,200,128]{2,1,0:T(8,128)(2,1)S(1)} %constant_dynamic-update-slice_fusion.blocks_ref), channel_id=1, source_target_pairs={{0,16},{16,0},{1,17},{17,1},{2,18},{18,2},{3,19},{19,3},{4,20},{20... | collective-permute-start | bytes 921608 | tf_op jit(solution)/shard_map/ppermute | solution.py:245
  25.9 0.1 pad_add_fusion.rank_ref
  25.9 0.8 %shard_map.30 = (bf16[16,96,256]{2,1,0:T(8,128)(2,1)S(1)}, f32[16,96,128]{2,1,0:T(8,128)S(1)}, f32[1,128]{1,0:T(1,128)S(1)}) custom-call(s32[2]{0:T(128)S(1)} %pad_add_fusion.rank_ref, bf16[2,200,128]{2,1,0:T(8,128)(2,1)S(1)} %pad_maximum_fusion.1.pair_ref, bf16[6,200,128]{2,1,0:T(8,128)(2,1)S(1)} %constant_dynamic-update-slice_fusion.blocks_ref), custom_call_target="tpu_custom_call" | custom-call | tf_op jit(solution)/shard_map/pallas_call | solution.py:251
  26.7 0.4 collective-permute-done.4.blocks_ref
  27.1 0.8 %shard_map.31 = (bf16[16,96,256]{2,1,0:T(8,128)(2,1)S(1)}, f32[16,96,128]{2,1,0:T(8,128)S(1)}) custom-call(s32[2]{0:T(128)S(1)} %pad_add_fusion.rank_ref, bf16[6,200,128]{2,1,0:T(8,128)(2,1)S(1)} %collective-permute-done.4.blocks_ref, bf16[2,200,128]{2,1,0:T(8,128)(2,1)S(1)} %collective-permute-done.2.last_ref, ...), custom_call_target="tpu_custom_call", output_to_operand_aliasing={{0}: (3, {}), {1}: (4, {})} | custom-call | tf_op jit(solution)/shard_map/pallas_call | solution.py:258
  27.8 0.0 all-to-all-done.left_ref
  27.9 2.0 %shard_map.32 = (f32[1536,1536]{1,0:T(8,128)S(1)}, f32[16,1,1664]{2,1,0:T(1,128)S(1)}) custom-call(bf16[16,96,256]{2,1,0:T(8,128)(2,1)S(1)} %get-tuple-element.23.right_ref, f32[16,96,128]{2,1,0:T(8,128)S(1)} %get-tuple-element.24.columns_ref, f32[1,128]{1,0:T(1,128)S(1)} %get-tuple-element.25.mass_ref, bf16[16,96,256]{2,1,0:T(8,128)(2,1)S(1)} %all-to-all-done.left_ref), custom_call_target="tpu_custom_call" | custom-call | tf_op jit(solution)/shard_map/pallas_call | solution.py:267
  29.8 13.7 %all_to_all.20.got_ref = f32[16,1,1664]{2,1,0:T(1,128)S(1)} all-to-all(f32[16,1,1664]{2,1,0:T(1,128)S(1)} %get-tuple-element.28), channel_id=1, replica_groups=mesh['x'=4,'yl'=2,'k'=2,'yh'=2,'z'=8] {'x','yl','yh'}, dimensions={0} | all-to-all | bytes 212992 | tf_op jit(solution)/shard_map/all_to_all | solution.py:274
  43.5 1.6 %shard_map.33 = f32[16,1,1664]{2,1,0:T(1,128)S(1)} custom-call(s32[2]{0:T(128)S(1)} %pad_add_fusion.rank_ref, f32[1536,1536]{1,0:T(8,128)S(1)} %get-tuple-element.27.kernel_ref, f32[16,1,1664]{2,1,0:T(1,128)S(1)} %all_to_all.20.got_ref), custom_call_target="tpu_custom_call" | custom-call | tf_op jit(solution)/shard_map/pallas_call | solution.py:275
  45.1 13.6 %all_to_all.21.got_ref = f32[16,1,1664]{2,1,0:T(1,128)S(1)} all-to-all(f32[16,1,1664]{2,1,0:T(1,128)S(1)} %shard_map.33), channel_id=1, replica_groups=mesh['x'=4,'yl'=2,'k'=2,'yh'=2,'z'=8] {'k','z'}, dimensions={0} | all-to-all | bytes 212992 | tf_op jit(solution)/shard_map/all_to_all | solution.py:283
  58.7 1.7 %shard_map.34 = (f32[16,1,128]{2,1,0:T(1,128)S(1)}, f32[1,96]{1,0:T(1,128)S(1)}) custom-call(s32[2]{0:T(128)S(1)} %pad_add_fusion.rank_ref, f32[1536,1536]{1,0:T(8,128)S(1)} %get-tuple-element.27.kernel_ref, f32[16,1,1664]{2,1,0:T(1,128)S(1)} %all_to_all.21.got_ref), custom_call_target="tpu_custom_call" | custom-call | tf_op jit(solution)/shard_map/pallas_call | solution.py:284
  60.3 9.2 %all_to_all.22 = f32[16,1,128]{2,1,0:T(1,128)S(1)} all-to-all(f32[16,1,128]{2,1,0:T(1,128)S(1)} %get-tuple-element.30), channel_id=1, replica_groups=mesh['x'=4,'yl'=2,'k'=2,'yh'=2,'z'=8] {'x','yl','yh'}, dimensions={0} | all-to-all | bytes 16384 | tf_op jit(solution)/shard_map/all_to_all | solution.py:292
  69.6 0.5 multiply_bitcast_fusion
  (5 shorter events, 0.1 us)
Async XLA Ops:
  0.9 4.4 %collective-permute-start = (bf16[200,128]{1,0:T(8,128)(2,1)S(1)}, bf16[200,128]{1,0:T(8,128)(2,1)S(1)}, u32[]{:S(2)}, u32[]{:S(2)}) collective-permute-start(bf16[200,128]{1,0:T(8,128)(2,1)S(1)} %shard_map.28.block_ref), channel_id=1, source_target_pairs={{0,16},{16,0},{1,17},{17,1},{2,18},{18,2},{3,19},{19,3},{4,20},{20... | collective-permute-start | bytes 153608 | tf_op jit(solution)/shard_map/ppermute | solution.py:239
  5.4 8.1 %collective-permute-start.1 = (bf16[2,200,128]{2,1,0:T(8,128)(2,1)S(1)}, bf16[2,200,128]{2,1,0:T(8,128)(2,1)S(1)}, u32[]{:S(2)}, u32[]{:S(2)}) collective-permute-start(bf16[2,200,128]{2,1,0:T(8,128)(2,1)S(1)} %pad_maximum_fusion.1.pair_ref), channel_id=1, source_target_pairs={{0,6},{1,7},{2,0},{3,1},{4,2},{5,3},{6,4},{7,5},{16,18},{17,19},{1... | collective-permute-start | bytes 307208 | tf_op jit(solution)/shard_map/ppermute | solution.py:48
  6.7 21.2 %all-to-all-start = ((bf16[16,96,256]{2,1,0:T(8,128)(2,1)}), bf16[16,96,256]{2,1,0:T(8,128)(2,1)S(1)}, u32[]{:S(2)}, u32[]{:S(2)}) async-start(bf16[16,96,256]{2,1,0:T(8,128)(2,1)} %shard_map.29), calls=%async_computation | async-start | bytes 1572864 | tf_op jit(solution)/shard_map/all_to_all | solution.py:246
  13.5 9.5 %collective-permute-start.3 = (bf16[4,200,128]{2,1,0:T(8,128)(2,1)S(1)}, bf16[4,200,128]{2,1,0:T(8,128)(2,1)S(1)}, u32[]{:S(2)}, u32[]{:S(2)}) collective-permute-start(bf16[4,200,128]{2,1,0:T(8,128)(2,1)S(1)} %pad_maximum_fusion), channel_id=1, source_target_pairs={{0,7},{1,0},{2,1},{3,2},{4,3},{5,4},{6,5},{7,6},{16,17},{17,18},{1... | collective-permute-start | bytes 614408 | tf_op jit(solution)/shard_map/ppermute | solution.py:48
  15.2 7.8 %collective-permute-start.2 = (bf16[2,200,128]{2,1,0:T(8,128)(2,1)S(1)}, bf16[2,200,128]{2,1,0:T(8,128)(2,1)S(1)}, u32[]{:S(2)}, u32[]{:S(2)}) collective-permute-start(bf16[2,200,128]{2,1,0:T(8,128)(2,1)S(1)} %collective-permute-done.1), channel_id=1, source_target_pairs={{0,6},{1,7},{2,0},{3,1},{4,2},{5,3},{6,4},{7,5},{16,18},{17,19},{1... | collective-permute-start | bytes 307208 | tf_op jit(solution)/shard_map/ppermute | solution.py:48
  23.0 4.1 %collective-permute-start.4 = (bf16[6,200,128]{2,1,0:T(8,128)(2,1)S(1)}, bf16[6,200,128]{2,1,0:T(8,128)(2,1)S(1)}, u32[]{:S(2)}, u32[]{:S(2)}) collective-permute-start(bf16[6,200,128]{2,1,0:T(8,128)(2,1)S(1)} %constant_dynamic-update-slice_fusion.blocks_ref), channel_id=1, source_target_pairs={{0,16},{16,0},{1,17},{17,1},{2,18},{18,2},{3,19},{19,3},{4,20},{20... | collective-permute-start | bytes 921608 | tf_op jit(solution)/shard_map/ppermute | solution.py:245
